TPU v7x, 512 devices: a whole 4x8x8 slice. The times are simulated.
512 devices in a mesh: ctx: 16 (over y, z_hi), ep: 32 (over z_lo, x, core).
Axes of the slice: x: 4, y: 8, z: 8 (z_hi: 2, z_lo: 4; z = z_hi * 4 + z_lo), core: 2. Of those that a mesh axis runs over, the one named last changes fastest.
Arguments:
- queries: bfloat16 [32, 96, 5120], P('ep', 'ctx'), may hold values from -200 to 200
- new_kv: bfloat16 [2, 32, 96, 1024], P(None, 'ep', 'ctx'), may hold values from -8 to 8
- cached_key_value: bfloat16 [2, 32, 4096, 1024], P(None, 'ep', 'ctx'), may hold values from -6 to 6
- cache_len: int32 [32], P('ep'), may hold values from 1 to 4096, 81920 in all
- residual: bfloat16 [32, 96, 5120], P('ep', 'ctx'), may hold values from -6 to 6
- norm_gain: bfloat16 [5120], replicated, may hold values from 0.099609375 to 1.8984375
- route_logit: float32 [32, 96], P('ep', 'ctx'), may hold values from 0.5 to 4
- route_id: int32 [32, 96, 1], P('ep'), may hold values from 0 to 15; in each aligned block of 96 rows (0 to 95, 96 to 191, ..., all dimensions but the last counted through in order) at most 12 rows name the same one
- w_gate: bfloat16 [32, 5120, 2048], P('ep', None, 'ctx'), may hold values from -0.078125 to 0.078125
- w_up: bfloat16 [32, 5120, 2048], P('ep', None, 'ctx'), may hold values from -0.078125 to 0.078125
- w_down: bfloat16 [32, 2048, 5120], P('ep', 'ctx'), may hold values from -0.1875 to 0.1875
Outputs:
- mixed_out: bfloat16 [32, 96, 5120], P('ep', 'ctx')
Inputs may be any that keep to these rules, and one draw needn't show every extreme that they name: `route_id`: in each request's 96 tokens at most 12 choose one expert.
All inputs are finite; a program needn't handle non-finite values. No bound on the sum of `cache_len` on one device may be relied on, other than what follows from the above.
Results may differ from a plain program's by a relative error of at most 0.023.
Values may be sent and summed in bfloat16 or wider, within the bound.
A program may use at most 64 MiB of HBM per device.

v0:
```python
import jax
import jax.numpy as jnp
from jax import lax
from jax.sharding import PartitionSpec as P

QUERY_HEADS = 40
KEY_VALUE_HEADS = 8
HEAD_WIDTH = 128


NEG_LARGE = -1e30


def from_behind(block, axis, distance):
    devices = range(lax.axis_size(axis))
    route = [((i - distance) % len(devices), i) for i in devices]
    return lax.ppermute(block, axis, route)


def merge_sums(left_sums, right_sums):
    top_left, total_left, weighted_left = left_sums
    top_right, total_right, weighted_right = right_sums
    top_score = jnp.maximum(top_left, top_right)
    factor_left = jnp.exp(top_left - top_score)
    factor_right = jnp.exp(top_right - top_score)
    weight_total = total_left * factor_left + total_right * factor_right
    request_row_count, head_count = factor_left.shape
    weighted = (
        weighted_left.reshape(request_row_count, head_count, HEAD_WIDTH) * factor_left[..., None]
    )
    weighted = (
        weighted
        + weighted_right.reshape(request_row_count, head_count, HEAD_WIDTH)
        * factor_right[..., None]
    )
    return (top_score, weight_total, weighted.reshape(request_row_count, head_count * HEAD_WIDTH))


def local_attention(
    query_row_block, query_index, key_row_block, value_row_block, cache_ok, new_key_index
):
    request_row_count = query_row_block.shape[0]
    query_group_width = QUERY_HEADS // KEY_VALUE_HEADS
    query_head_rows = query_row_block.reshape(
        request_row_count, KEY_VALUE_HEADS, query_group_width, HEAD_WIDTH
    )
    key_head_rows = key_row_block.reshape(-1, KEY_VALUE_HEADS, HEAD_WIDTH)
    value_head_rows = value_row_block.reshape(-1, KEY_VALUE_HEADS, HEAD_WIDTH)
    scores = jnp.einsum(
        "tgjd,lgd->gjtl", query_head_rows, key_head_rows, preferred_element_type=jnp.float32
    ) * HEAD_WIDTH ** (-0.5)
    new_ok = new_key_index[None, :] <= query_index[:, None]
    cache_part = jnp.broadcast_to(cache_ok[None, :], (request_row_count, cache_ok.shape[0]))
    allowed = jnp.concatenate([cache_part, new_ok], axis=1)
    scores = jnp.where(allowed, scores, NEG_LARGE)
    top_score = jnp.max(scores, axis=-1)
    weights = jnp.where(allowed, jnp.exp(scores - top_score[..., None]), 0.0)
    weight_total = jnp.sum(weights, axis=-1)
    weighted = jnp.einsum(
        "gjtl,lgd->tgjd",
        weights.astype(jnp.bfloat16),
        value_head_rows,
        preferred_element_type=jnp.float32,
    )
    top_rows = jnp.transpose(top_score, (2, 0, 1)).reshape(request_row_count, QUERY_HEADS)
    total_rows = jnp.transpose(weight_total, (2, 0, 1)).reshape(request_row_count, QUERY_HEADS)
    return (top_rows, total_rows, weighted.reshape(request_row_count, QUERY_HEADS * HEAD_WIDTH))


def body(
    queries,
    new_kv,
    cached_key_value,
    cache_len,
    residual,
    norm_gain,
    route_logit,
    route_id,
    w_gate,
    w_up,
    w_down,
):
    ctx_size = lax.axis_size("ctx")
    position = lax.axis_index("ctx")
    tok_dev = queries.shape[1]
    cache_dev = cached_key_value.shape[2]
    key_row_block = jnp.concatenate([cached_key_value[0, 0], new_kv[0, 0]], axis=0)
    value_row_block = jnp.concatenate([cached_key_value[1, 0], new_kv[1, 0]], axis=0)
    cache_ok = position * cache_dev + jnp.arange(cache_dev, dtype=jnp.int32) < cache_len[0]
    local_index = jnp.arange(tok_dev, dtype=jnp.int32)
    new_key_index = position * tok_dev + local_index

    def attend(query_row_block, query_index):
        return local_attention(
            query_row_block, query_index, key_row_block, value_row_block, cache_ok, new_key_index
        )

    def carry_sums(running):
        return (
            from_behind(running[0].astype(jnp.bfloat16), "ctx", 1).astype(jnp.float32),
            from_behind(running[1].astype(jnp.bfloat16), "ctx", 1).astype(jnp.float32),
            from_behind(running[2].astype(jnp.bfloat16), "ctx", 1).astype(jnp.float32),
        )

    def pass_turn(turn_index, moving):
        query_row_block, running = moving
        query_row_block = from_behind(query_row_block, "ctx", 1)
        running = carry_sums(running)
        anchor = (position - turn_index) % ctx_size
        running = merge_sums(running, attend(query_row_block, anchor * tok_dev + local_index))
        return (query_row_block, running)

    own_rows = queries[0]
    unused, running = lax.fori_loop(
        1, ctx_size, pass_turn, (own_rows, attend(own_rows, new_key_index))
    )
    top_score, weight_total, weighted = carry_sums(running)
    attended = (
        weighted.reshape(tok_dev, QUERY_HEADS, HEAD_WIDTH) / weight_total[..., None]
    ).reshape(tok_dev, QUERY_HEADS * HEAD_WIDTH)
    hidden_state = (residual[0].astype(jnp.float32) + attended).astype(jnp.bfloat16)
    hidden_f32 = hidden_state.astype(jnp.float32)
    inv_rms = lax.rsqrt(jnp.mean(hidden_f32 * hidden_f32, axis=-1, keepdims=True) + 1e-05)
    expert_in = (
        hidden_f32
        * inv_rms
        * norm_gain.astype(jnp.float32)
        * jax.nn.sigmoid(route_logit[0])[:, None]
    ).astype(jnp.bfloat16)
    request_rows = lax.all_gather(expert_in, "ctx", axis=0, tiled=True)
    row_total = request_rows.shape[0]
    model_width = request_rows.shape[1]
    fleet_size = lax.axis_size("ep")
    experts = fleet_size // 2
    capacity = 2 * row_total // experts
    expert_ids = route_id[0, :, 0]
    one_hot = (expert_ids[:, None] == jnp.arange(experts, dtype=jnp.int32)).astype(jnp.int32)
    slot_rank = jnp.sum((jnp.cumsum(one_hot, axis=0) - one_hot) * one_hot, axis=-1)
    slot_row = expert_ids * capacity + slot_rank
    packed = (
        jnp.zeros((experts * capacity, model_width), jnp.bfloat16).at[slot_row].set(request_rows)
    )
    gate_cols = w_gate[0]
    up_cols = w_up[0]
    down_rows = w_down[0]
    outgoing = jnp.repeat(packed.reshape(experts, capacity, model_width), 2, axis=0)
    token_rows = lax.all_to_all(outgoing, "ep", split_axis=0, concat_axis=0, tiled=True)
    flat_rows = token_rows.reshape(-1, model_width)
    gate_out = jnp.dot(flat_rows, gate_cols, preferred_element_type=jnp.float32)
    up_out = jnp.dot(flat_rows, up_cols, preferred_element_type=jnp.float32)
    act = (jax.nn.silu(gate_out) * up_out).astype(jnp.bfloat16)
    products = jnp.dot(act, down_rows, preferred_element_type=jnp.float32).astype(jnp.bfloat16)
    returned = lax.all_to_all(
        products.reshape(token_rows.shape), "ep", split_axis=0, concat_axis=0, tiled=True
    )
    slot_sums = jnp.sum(
        returned.reshape(experts, 2, capacity, model_width).astype(jnp.float32), axis=1
    )
    routed = slot_sums.reshape(experts * capacity, model_width)[slot_row]
    summed = lax.psum_scatter(
        routed.astype(jnp.bfloat16), "ctx", scatter_dimension=0, tiled=True
    ).astype(jnp.float32)
    mixed_out = (hidden_f32 + summed).astype(jnp.bfloat16)
    return mixed_out[None]


def solution(mesh):
    placed = (
        P("ep", "ctx", None),
        P(None, "ep", "ctx", None),
        P(None, "ep", "ctx", None),
        P("ep"),
        P("ep", "ctx", None),
        P(),
        P("ep", "ctx"),
        P("ep", None, None),
        P("ep", None, "ctx"),
        P("ep", None, "ctx"),
        P("ep", "ctx", None),
    )
    return jax.shard_map(
        body, mesh=mesh, in_specs=placed, out_specs=P("ep", "ctx", None), check_vma=False
    )
```

profile of v0, /device:TPU:22, one launch (start us, length us, event | category | flops | bytes accessed | tf_op | source)
XLA Modules:
  0.0 926.9 jit_solution(6909143006806885004)
XLA Ops:
  12.6 409.0 %while.22 = (s32[]{:T(128)}, bf16[6,5120]{1,0:T(8,128)(2,1)S(1)}, bf16[6,40]{1,0:T(8,128)(2,1)S(1)}, bf16[6,40]{1,0:T(8,128)(2,1)S(1)}, bf16[6,5120]{1,0:T(8,128...) while((s32[]{:T(128)}, bf16[6,5120]{1,0:T(8,128)(2,1)S(1)}, ...), condition=%wide.region_5.6_spmd.clone, body=%wide.region_2.5_spmd.clone.sunk | while | flops 32918148 | bytes 7703703 | solution.py:114
  12.6 11.0 %collective-permute-start = (bf16[6,5120]{1,0:T(8,128)(2,1)S(1)}, bf16[6,5120]{1,0:T(8,128)(2,1)S(1)}, u32[]{:S(2)}, u32[]{:S(2)}) collective-permute-start(bf16[6,5120]{1,0:T(8,128)(2,1)S(1)} %get-tuple-element.478), channel_id=1, source_target_pairs={{480,0},{0,32},{32,64},{64,96},{96,128},{128,160},{160,192},{192,2... | collective-permute-start | bytes 184328 | tf_op jit(solution)/shard_map/while/body/eval_jaxpr/ppermute | solution.py:17
  25.6 8.8 collective-permute-start.2
  38.8 7.6 collective-permute-done.3
  49.0 9.6 %collective-permute-start.1 = (bf16[6,40]{1,0:T(8,128)(2,1)S(1)}, bf16[6,40]{1,0:T(8,128)(2,1)S(1)}, u32[]{:S(2)}, u32[]{:S(2)}) collective-permute-start(bf16[6,40]{1,0:T(8,128)(2,1)S(1)} %get-tuple-element.480), channel_id=1, source_target_pairs={{480,0},{0,32},{32,64},{64,96},{96,128},{128,160},{160,192},{192,2... | collective-permute-start | bytes 1448 | tf_op jit(solution)/shard_map/while/body/eval_jaxpr/ppermute | solution.py:17
  60.5 9.1 collective-permute-start.3
  72.4 7.9 collective-permute-start
  83.7 5.0 collective-permute-start.2
  103.8 6.9 collective-permute-start.1
  113.2 7.6 collective-permute-start.3
  125.2 6.8 collective-permute-start
  134.5 8.1 collective-permute-start.2
  157.5 7.2 collective-permute-start.1
  166.7 11.8 %collective-permute-start.3 = (bf16[6,5120]{1,0:T(8,128)(2,1)S(1)}, bf16[6,5120]{1,0:T(8,128)(2,1)S(1)}, u32[]{:S(2)}, u32[]{:S(2)}) collective-permute-start(bf16[6,5120]{1,0:T(8,128)(2,1)S(1)} %get-tuple-element.481), channel_id=1, source_target_pairs={{480,0},{0,32},{32,64},{64,96},{96,128},{128,160},{160,192},{192,2... | collective-permute-start | bytes 184328 | tf_op jit(solution)/shard_map/while/body/eval_jaxpr/ppermute | solution.py:17
  181.0 7.8 collective-permute-start
  191.7 6.6 collective-permute-start.2
  204.4 5.1 collective-permute-done.3
  212.3 6.9 collective-permute-start.1
  223.1 6.2 collective-permute-start.3
  234.3 5.6 collective-permute-start
  242.9 5.8 collective-permute-start.2
  264.5 6.2 collective-permute-start.1
  274.8 7.2 collective-permute-start.3
  286.1 6.3 collective-permute-start
  292.3 5.6 collective-permute-start.1
  297.9 5.7 collective-permute-start.2
  303.6 5.7 collective-permute-start.3
  319.7 6.6 collective-permute-start.1
  329.9 7.3 collective-permute-start.3
  341.2 6.7 collective-permute-start
  350.8 6.6 collective-permute-start.2
  357.4 6.9 collective-permute-start.3
  368.6 7.0 collective-permute-start
  381.4 5.8 collective-permute-start.3
  401.9 7.4 collective-permute-start.2
  426.6 6.3 collective-permute-start.4
  438.5 65.6 %all-gather = bf16[16,6,5120]{2,1,0:T(8,128)(2,1)S(1)} all-gather(bf16[1,6,5120]{2,1,0:T(8,128)(2,1)S(1)} %fusion.63), channel_id=1, replica_groups=mesh['ctx'=16,'ep'=32] {'ctx'}, dimensions={0}, use_global_device_ids=true | all-gather | bytes 1044480 | tf_op jit(solution)/shard_map/all_gather | solution.py:130
  513.0 141.7 %all_to_all.10 = bf16[32,12,5120]{2,1,0:T(8,128)(2,1)} all-to-all(bf16[32,12,5120]{2,1,0:T(8,128)(2,1)S(1)} %bitcast.157), channel_id=1, replica_groups=mesh['ctx'=16,'ep'=32] {'ep'}, dimensions={0} | all-to-all | bytes 7864320 | tf_op jit(solution)/shard_map/all_to_all | solution.py:147
  654.8 7.2 reshape.204
  665.3 8.6 convolution_convert_fusion
  673.9 6.9 reshape.205
  680.8 6.0 all-to-all-start.1
  686.8 115.9 %all-to-all-done.1 = bf16[32,12,5120]{2,1,0:T(8,128)(2,1)} async-done(((bf16[32,12,5120]{2,1,0:T(8,128)(2,1)}), bf16[32,12,5120]{2,1,0:T(8,128)(2,1)}, u32[]{:S(2)}, u32[]{:S(2)}) %all-to-all-start.1) | async-done | bytes 3932192 | tf_op jit(solution)/shard_map/all_to_all | solution.py:153
  802.8 6.1 convert_reduce_fusion
  813.6 73.6 %fusion.6 = bf16[8,5120]{1,0:T(8,128)(2,1)S(1)} fusion(bf16[96,5120]{1,0:T(8,128)(2,1)} %gather_fusion), kind=kCustom, calls=%all-reduce-scatter | all-reduce-scatter fusion | flops 655361 | bytes 1067008
  887.2 8.9 collective-permute-start.6
  896.1 10.0 %collective-permute-start.7 = (bf16[8,5120]{1,0:T(8,128)(2,1)S(1)}, bf16[8,5120]{1,0:T(8,128)(2,1)S(1)}, u32[]{:S(2)}, u32[]{:S(2)}) collective-permute-start(bf16[8,5120]{1,0:T(8,128)(2,1)S(1)} %fusion.6), channel_id=1, source_target_pairs={{0,64},{32,96},{64,128},{96,160},{128,192},{160,224},{192,256},{22... | collective-permute-start | bytes 245768
  906.1 11.6 %collective-permute-start.8 = (bf16[8,5120]{1,0:T(8,128)(2,1)S(1)}, bf16[8,5120]{1,0:T(8,128)(2,1)S(1)}, u32[]{:S(2)}, u32[]{:S(2)}) collective-permute-start(bf16[8,5120]{1,0:T(8,128)(2,1)S(1)} %fusion.6), channel_id=1, source_target_pairs={{0,96},{32,128},{64,160},{96,192},{128,224},{160,256},{192,288},{2... | collective-permute-start | bytes 245768
  (485 shorter events, 211.5 us)
Async XLA Ops:
  12.6 24.9 %collective-permute-start = (bf16[6,5120]{1,0:T(8,128)(2,1)S(1)}, bf16[6,5120]{1,0:T(8,128)(2,1)S(1)}, u32[]{:S(2)}, u32[]{:S(2)}) collective-permute-start(bf16[6,5120]{1,0:T(8,128)(2,1)S(1)} %get-tuple-element.478), channel_id=1, source_target_pairs={{480,0},{0,32},{32,64},{64,96},{96,128},{128,160},{160,192},{192,2... | collective-permute-start | bytes 184328 | tf_op jit(solution)/shard_map/while/body/eval_jaxpr/ppermute | solution.py:17
  23.7 15.0 %collective-permute-start.1 = (bf16[6,40]{1,0:T(8,128)(2,1)S(1)}, bf16[6,40]{1,0:T(8,128)(2,1)S(1)}, u32[]{:S(2)}, u32[]{:S(2)}) collective-permute-start(bf16[6,40]{1,0:T(8,128)(2,1)S(1)} %get-tuple-element.480), channel_id=1, source_target_pairs={{480,0},{0,32},{32,64},{64,96},{96,128},{128,160},{160,192},{192,2... | collective-permute-start | bytes 1448 | tf_op jit(solution)/shard_map/while/body/eval_jaxpr/ppermute | solution.py:17
  25.6 13.1 %collective-permute-start.2 = (bf16[6,40]{1,0:T(8,128)(2,1)S(1)}, bf16[6,40]{1,0:T(8,128)(2,1)S(1)}, u32[]{:S(2)}, u32[]{:S(2)}) collective-permute-start(bf16[6,40]{1,0:T(8,128)(2,1)S(1)} %get-tuple-element.479), channel_id=1, source_target_pairs={{480,0},{0,32},{32,64},{64,96},{96,128},{128,160},{160,192},{192,2... | collective-permute-start | bytes 1448 | tf_op jit(solution)/shard_map/while/body/eval_jaxpr/ppermute | solution.py:17
  46.6 24.2 %collective-permute-start = (bf16[6,5120]{1,0:T(8,128)(2,1)S(1)}, bf16[6,5120]{1,0:T(8,128)(2,1)S(1)}, u32[]{:S(2)}, u32[]{:S(2)}) collective-permute-start(bf16[6,5120]{1,0:T(8,128)(2,1)S(1)} %get-tuple-element.478), channel_id=1, source_target_pairs={{480,0},{0,32},{32,64},{64,96},{96,128},{128,160},{160,192},{192,2... | collective-permute-start | bytes 184328 | tf_op jit(solution)/shard_map/while/body/eval_jaxpr/ppermute | solution.py:17
  49.0 22.9 %collective-permute-start.1 = (bf16[6,40]{1,0:T(8,128)(2,1)S(1)}, bf16[6,40]{1,0:T(8,128)(2,1)S(1)}, u32[]{:S(2)}, u32[]{:S(2)}) collective-permute-start(bf16[6,40]{1,0:T(8,128)(2,1)S(1)} %get-tuple-element.480), channel_id=1, source_target_pairs={{480,0},{0,32},{32,64},{64,96},{96,128},{128,160},{160,192},{192,2... | collective-permute-start | bytes 1448 | tf_op jit(solution)/shard_map/while/body/eval_jaxpr/ppermute | solution.py:17
  58.6 13.3 %collective-permute-start.2 = (bf16[6,40]{1,0:T(8,128)(2,1)S(1)}, bf16[6,40]{1,0:T(8,128)(2,1)S(1)}, u32[]{:S(2)}, u32[]{:S(2)}) collective-permute-start(bf16[6,40]{1,0:T(8,128)(2,1)S(1)} %get-tuple-element.479), channel_id=1, source_target_pairs={{480,0},{0,32},{32,64},{64,96},{96,128},{128,160},{160,192},{192,2... | collective-permute-start | bytes 1448 | tf_op jit(solution)/shard_map/while/body/eval_jaxpr/ppermute | solution.py:17
  72.4 22.1 %collective-permute-start = (bf16[6,5120]{1,0:T(8,128)(2,1)S(1)}, bf16[6,5120]{1,0:T(8,128)(2,1)S(1)}, u32[]{:S(2)}, u32[]{:S(2)}) collective-permute-start(bf16[6,5120]{1,0:T(8,128)(2,1)S(1)} %get-tuple-element.478), channel_id=1, source_target_pairs={{480,0},{0,32},{32,64},{64,96},{96,128},{128,160},{160,192},{192,2... | collective-permute-start | bytes 184328 | tf_op jit(solution)/shard_map/while/body/eval_jaxpr/ppermute | solution.py:17
  80.3 15.4 %collective-permute-start.1 = (bf16[6,40]{1,0:T(8,128)(2,1)S(1)}, bf16[6,40]{1,0:T(8,128)(2,1)S(1)}, u32[]{:S(2)}, u32[]{:S(2)}) collective-permute-start(bf16[6,40]{1,0:T(8,128)(2,1)S(1)} %get-tuple-element.480), channel_id=1, source_target_pairs={{480,0},{0,32},{32,64},{64,96},{96,128},{128,160},{160,192},{192,2... | collective-permute-start | bytes 1448 | tf_op jit(solution)/shard_map/while/body/eval_jaxpr/ppermute | solution.py:17
  100.2 21.7 %collective-permute-start = (bf16[6,5120]{1,0:T(8,128)(2,1)S(1)}, bf16[6,5120]{1,0:T(8,128)(2,1)S(1)}, u32[]{:S(2)}, u32[]{:S(2)}) collective-permute-start(bf16[6,5120]{1,0:T(8,128)(2,1)S(1)} %get-tuple-element.478), channel_id=1, source_target_pairs={{480,0},{0,32},{32,64},{64,96},{96,128},{128,160},{160,192},{192,2... | collective-permute-start | bytes 184328 | tf_op jit(solution)/shard_map/while/body/eval_jaxpr/ppermute | solution.py:17
  103.8 19.3 %collective-permute-start.1 = (bf16[6,40]{1,0:T(8,128)(2,1)S(1)}, bf16[6,40]{1,0:T(8,128)(2,1)S(1)}, u32[]{:S(2)}, u32[]{:S(2)}) collective-permute-start(bf16[6,40]{1,0:T(8,128)(2,1)S(1)} %get-tuple-element.480), channel_id=1, source_target_pairs={{480,0},{0,32},{32,64},{64,96},{96,128},{128,160},{160,192},{192,2... | collective-permute-start | bytes 1448 | tf_op jit(solution)/shard_map/while/body/eval_jaxpr/ppermute | solution.py:17
  110.7 12.4 %collective-permute-start.2 = (bf16[6,40]{1,0:T(8,128)(2,1)S(1)}, bf16[6,40]{1,0:T(8,128)(2,1)S(1)}, u32[]{:S(2)}, u32[]{:S(2)}) collective-permute-start(bf16[6,40]{1,0:T(8,128)(2,1)S(1)} %get-tuple-element.479), channel_id=1, source_target_pairs={{480,0},{0,32},{32,64},{64,96},{96,128},{128,160},{160,192},{192,2... | collective-permute-start | bytes 1448 | tf_op jit(solution)/shard_map/while/body/eval_jaxpr/ppermute | solution.py:17
  125.2 23.1 %collective-permute-start = (bf16[6,5120]{1,0:T(8,128)(2,1)S(1)}, bf16[6,5120]{1,0:T(8,128)(2,1)S(1)}, u32[]{:S(2)}, u32[]{:S(2)}) collective-permute-start(bf16[6,5120]{1,0:T(8,128)(2,1)S(1)} %get-tuple-element.478), channel_id=1, source_target_pairs={{480,0},{0,32},{32,64},{64,96},{96,128},{128,160},{160,192},{192,2... | collective-permute-start | bytes 184328 | tf_op jit(solution)/shard_map/while/body/eval_jaxpr/ppermute | solution.py:17
  132.0 17.5 %collective-permute-start.1 = (bf16[6,40]{1,0:T(8,128)(2,1)S(1)}, bf16[6,40]{1,0:T(8,128)(2,1)S(1)}, u32[]{:S(2)}, u32[]{:S(2)}) collective-permute-start(bf16[6,40]{1,0:T(8,128)(2,1)S(1)} %get-tuple-element.480), channel_id=1, source_target_pairs={{480,0},{0,32},{32,64},{64,96},{96,128},{128,160},{160,192},{192,2... | collective-permute-start | bytes 1448 | tf_op jit(solution)/shard_map/while/body/eval_jaxpr/ppermute | solution.py:17
  134.5 15.0 %collective-permute-start.2 = (bf16[6,40]{1,0:T(8,128)(2,1)S(1)}, bf16[6,40]{1,0:T(8,128)(2,1)S(1)}, u32[]{:S(2)}, u32[]{:S(2)}) collective-permute-start(bf16[6,40]{1,0:T(8,128)(2,1)S(1)} %get-tuple-element.479), channel_id=1, source_target_pairs={{480,0},{0,32},{32,64},{64,96},{96,128},{128,160},{160,192},{192,2... | collective-permute-start | bytes 1448 | tf_op jit(solution)/shard_map/while/body/eval_jaxpr/ppermute | solution.py:17
  154.5 25.1 %collective-permute-start = (bf16[6,5120]{1,0:T(8,128)(2,1)S(1)}, bf16[6,5120]{1,0:T(8,128)(2,1)S(1)}, u32[]{:S(2)}, u32[]{:S(2)}) collective-permute-start(bf16[6,5120]{1,0:T(8,128)(2,1)S(1)} %get-tuple-element.478), channel_id=1, source_target_pairs={{480,0},{0,32},{32,64},{64,96},{96,128},{128,160},{160,192},{192,2... | collective-permute-start | bytes 184328 | tf_op jit(solution)/shard_map/while/body/eval_jaxpr/ppermute | solution.py:17
  157.5 23.2 %collective-permute-start.1 = (bf16[6,40]{1,0:T(8,128)(2,1)S(1)}, bf16[6,40]{1,0:T(8,128)(2,1)S(1)}, u32[]{:S(2)}, u32[]{:S(2)}) collective-permute-start(bf16[6,40]{1,0:T(8,128)(2,1)S(1)} %get-tuple-element.480), channel_id=1, source_target_pairs={{480,0},{0,32},{32,64},{64,96},{96,128},{128,160},{160,192},{192,2... | collective-permute-start | bytes 1448 | tf_op jit(solution)/shard_map/while/body/eval_jaxpr/ppermute | solution.py:17
  164.7 16.0 %collective-permute-start.2 = (bf16[6,40]{1,0:T(8,128)(2,1)S(1)}, bf16[6,40]{1,0:T(8,128)(2,1)S(1)}, u32[]{:S(2)}, u32[]{:S(2)}) collective-permute-start(bf16[6,40]{1,0:T(8,128)(2,1)S(1)} %get-tuple-element.479), channel_id=1, source_target_pairs={{480,0},{0,32},{32,64},{64,96},{96,128},{128,160},{160,192},{192,2... | collective-permute-start | bytes 1448 | tf_op jit(solution)/shard_map/while/body/eval_jaxpr/ppermute | solution.py:17
  166.7 14.3 %collective-permute-start.3 = (bf16[6,5120]{1,0:T(8,128)(2,1)S(1)}, bf16[6,5120]{1,0:T(8,128)(2,1)S(1)}, u32[]{:S(2)}, u32[]{:S(2)}) collective-permute-start(bf16[6,5120]{1,0:T(8,128)(2,1)S(1)} %get-tuple-element.481), channel_id=1, source_target_pairs={{480,0},{0,32},{32,64},{64,96},{96,128},{128,160},{160,192},{192,2... | collective-permute-start | bytes 184328 | tf_op jit(solution)/shard_map/while/body/eval_jaxpr/ppermute | solution.py:17
  181.0 22.0 %collective-permute-start = (bf16[6,5120]{1,0:T(8,128)(2,1)S(1)}, bf16[6,5120]{1,0:T(8,128)(2,1)S(1)}, u32[]{:S(2)}, u32[]{:S(2)}) collective-permute-start(bf16[6,5120]{1,0:T(8,128)(2,1)S(1)} %get-tuple-element.478), channel_id=1, source_target_pairs={{480,0},{0,32},{32,64},{64,96},{96,128},{128,160},{160,192},{192,2... | collective-permute-start | bytes 184328 | tf_op jit(solution)/shard_map/while/body/eval_jaxpr/ppermute | solution.py:17
  188.8 15.4 %collective-permute-start.1 = (bf16[6,40]{1,0:T(8,128)(2,1)S(1)}, bf16[6,40]{1,0:T(8,128)(2,1)S(1)}, u32[]{:S(2)}, u32[]{:S(2)}) collective-permute-start(bf16[6,40]{1,0:T(8,128)(2,1)S(1)} %get-tuple-element.480), channel_id=1, source_target_pairs={{480,0},{0,32},{32,64},{64,96},{96,128},{128,160},{160,192},{192,2... | collective-permute-start | bytes 1448 | tf_op jit(solution)/shard_map/while/body/eval_jaxpr/ppermute | solution.py:17
  191.7 12.6 %collective-permute-start.2 = (bf16[6,40]{1,0:T(8,128)(2,1)S(1)}, bf16[6,40]{1,0:T(8,128)(2,1)S(1)}, u32[]{:S(2)}, u32[]{:S(2)}) collective-permute-start(bf16[6,40]{1,0:T(8,128)(2,1)S(1)} %get-tuple-element.479), channel_id=1, source_target_pairs={{480,0},{0,32},{32,64},{64,96},{96,128},{128,160},{160,192},{192,2... | collective-permute-start | bytes 1448 | tf_op jit(solution)/shard_map/while/body/eval_jaxpr/ppermute | solution.py:17
  209.6 20.8 %collective-permute-start = (bf16[6,5120]{1,0:T(8,128)(2,1)S(1)}, bf16[6,5120]{1,0:T(8,128)(2,1)S(1)}, u32[]{:S(2)}, u32[]{:S(2)}) collective-permute-start(bf16[6,5120]{1,0:T(8,128)(2,1)S(1)} %get-tuple-element.478), channel_id=1, source_target_pairs={{480,0},{0,32},{32,64},{64,96},{96,128},{128,160},{160,192},{192,2... | collective-permute-start | bytes 184328 | tf_op jit(solution)/shard_map/while/body/eval_jaxpr/ppermute | solution.py:17
  212.3 19.3 %collective-permute-start.1 = (bf16[6,40]{1,0:T(8,128)(2,1)S(1)}, bf16[6,40]{1,0:T(8,128)(2,1)S(1)}, u32[]{:S(2)}, u32[]{:S(2)}) collective-permute-start(bf16[6,40]{1,0:T(8,128)(2,1)S(1)} %get-tuple-element.480), channel_id=1, source_target_pairs={{480,0},{0,32},{32,64},{64,96},{96,128},{128,160},{160,192},{192,2... | collective-permute-start | bytes 1448 | tf_op jit(solution)/shard_map/while/body/eval_jaxpr/ppermute | solution.py:17
  219.2 12.3 %collective-permute-start.2 = (bf16[6,40]{1,0:T(8,128)(2,1)S(1)}, bf16[6,40]{1,0:T(8,128)(2,1)S(1)}, u32[]{:S(2)}, u32[]{:S(2)}) collective-permute-start(bf16[6,40]{1,0:T(8,128)(2,1)S(1)} %get-tuple-element.479), channel_id=1, source_target_pairs={{480,0},{0,32},{32,64},{64,96},{96,128},{128,160},{160,192},{192,2... | collective-permute-start | bytes 1448 | tf_op jit(solution)/shard_map/while/body/eval_jaxpr/ppermute | solution.py:17
  234.3 20.2 %collective-permute-start = (bf16[6,5120]{1,0:T(8,128)(2,1)S(1)}, bf16[6,5120]{1,0:T(8,128)(2,1)S(1)}, u32[]{:S(2)}, u32[]{:S(2)}) collective-permute-start(bf16[6,5120]{1,0:T(8,128)(2,1)S(1)} %get-tuple-element.478), channel_id=1, source_target_pairs={{480,0},{0,32},{32,64},{64,96},{96,128},{128,160},{160,192},{192,2... | collective-permute-start | bytes 184328 | tf_op jit(solution)/shard_map/while/body/eval_jaxpr/ppermute | solution.py:17
  239.9 15.7 %collective-permute-start.1 = (bf16[6,40]{1,0:T(8,128)(2,1)S(1)}, bf16[6,40]{1,0:T(8,128)(2,1)S(1)}, u32[]{:S(2)}, u32[]{:S(2)}) collective-permute-start(bf16[6,40]{1,0:T(8,128)(2,1)S(1)} %get-tuple-element.480), channel_id=1, source_target_pairs={{480,0},{0,32},{32,64},{64,96},{96,128},{128,160},{160,192},{192,2... | collective-permute-start | bytes 1448 | tf_op jit(solution)/shard_map/while/body/eval_jaxpr/ppermute | solution.py:17
  242.9 12.7 %collective-permute-start.2 = (bf16[6,40]{1,0:T(8,128)(2,1)S(1)}, bf16[6,40]{1,0:T(8,128)(2,1)S(1)}, u32[]{:S(2)}, u32[]{:S(2)}) collective-permute-start(bf16[6,40]{1,0:T(8,128)(2,1)S(1)} %get-tuple-element.479), channel_id=1, source_target_pairs={{480,0},{0,32},{32,64},{64,96},{96,128},{128,160},{160,192},{192,2... | collective-permute-start | bytes 1448 | tf_op jit(solution)/shard_map/while/body/eval_jaxpr/ppermute | solution.py:17
  260.0 23.1 %collective-permute-start = (bf16[6,5120]{1,0:T(8,128)(2,1)S(1)}, bf16[6,5120]{1,0:T(8,128)(2,1)S(1)}, u32[]{:S(2)}, u32[]{:S(2)}) collective-permute-start(bf16[6,5120]{1,0:T(8,128)(2,1)S(1)} %get-tuple-element.478), channel_id=1, source_target_pairs={{480,0},{0,32},{32,64},{64,96},{96,128},{128,160},{160,192},{192,2... | collective-permute-start | bytes 184328 | tf_op jit(solution)/shard_map/while/body/eval_jaxpr/ppermute | solution.py:17
  264.5 19.7 %collective-permute-start.1 = (bf16[6,40]{1,0:T(8,128)(2,1)S(1)}, bf16[6,40]{1,0:T(8,128)(2,1)S(1)}, u32[]{:S(2)}, u32[]{:S(2)}) collective-permute-start(bf16[6,40]{1,0:T(8,128)(2,1)S(1)} %get-tuple-element.480), channel_id=1, source_target_pairs={{480,0},{0,32},{32,64},{64,96},{96,128},{128,160},{160,192},{192,2... | collective-permute-start | bytes 1448 | tf_op jit(solution)/shard_map/while/body/eval_jaxpr/ppermute | solution.py:17
  270.7 13.6 %collective-permute-start.2 = (bf16[6,40]{1,0:T(8,128)(2,1)S(1)}, bf16[6,40]{1,0:T(8,128)(2,1)S(1)}, u32[]{:S(2)}, u32[]{:S(2)}) collective-permute-start(bf16[6,40]{1,0:T(8,128)(2,1)S(1)} %get-tuple-element.479), channel_id=1, source_target_pairs={{480,0},{0,32},{32,64},{64,96},{96,128},{128,160},{160,192},{192,2... | collective-permute-start | bytes 1448 | tf_op jit(solution)/shard_map/while/body/eval_jaxpr/ppermute | solution.py:17
  286.1 24.4 %collective-permute-start = (bf16[6,5120]{1,0:T(8,128)(2,1)S(1)}, bf16[6,5120]{1,0:T(8,128)(2,1)S(1)}, u32[]{:S(2)}, u32[]{:S(2)}) collective-permute-start(bf16[6,5120]{1,0:T(8,128)(2,1)S(1)} %get-tuple-element.478), channel_id=1, source_target_pairs={{480,0},{0,32},{32,64},{64,96},{96,128},{128,160},{160,192},{192,2... | collective-permute-start | bytes 184328 | tf_op jit(solution)/shard_map/while/body/eval_jaxpr/ppermute | solution.py:17
  292.3 19.3 %collective-permute-start.1 = (bf16[6,40]{1,0:T(8,128)(2,1)S(1)}, bf16[6,40]{1,0:T(8,128)(2,1)S(1)}, u32[]{:S(2)}, u32[]{:S(2)}) collective-permute-start(bf16[6,40]{1,0:T(8,128)(2,1)S(1)} %get-tuple-element.480), channel_id=1, source_target_pairs={{480,0},{0,32},{32,64},{64,96},{96,128},{128,160},{160,192},{192,2... | collective-permute-start | bytes 1448 | tf_op jit(solution)/shard_map/while/body/eval_jaxpr/ppermute | solution.py:17
  297.9 13.7 %collective-permute-start.2 = (bf16[6,40]{1,0:T(8,128)(2,1)S(1)}, bf16[6,40]{1,0:T(8,128)(2,1)S(1)}, u32[]{:S(2)}, u32[]{:S(2)}) collective-permute-start(bf16[6,40]{1,0:T(8,128)(2,1)S(1)} %get-tuple-element.479), channel_id=1, source_target_pairs={{480,0},{0,32},{32,64},{64,96},{96,128},{128,160},{160,192},{192,2... | collective-permute-start | bytes 1448 | tf_op jit(solution)/shard_map/while/body/eval_jaxpr/ppermute | solution.py:17
  314.8 23.5 %collective-permute-start = (bf16[6,5120]{1,0:T(8,128)(2,1)S(1)}, bf16[6,5120]{1,0:T(8,128)(2,1)S(1)}, u32[]{:S(2)}, u32[]{:S(2)}) collective-permute-start(bf16[6,5120]{1,0:T(8,128)(2,1)S(1)} %get-tuple-element.478), channel_id=1, source_target_pairs={{480,0},{0,32},{32,64},{64,96},{96,128},{128,160},{160,192},{192,2... | collective-permute-start | bytes 184328 | tf_op jit(solution)/shard_map/while/body/eval_jaxpr/ppermute | solution.py:17
  319.7 19.8 %collective-permute-start.1 = (bf16[6,40]{1,0:T(8,128)(2,1)S(1)}, bf16[6,40]{1,0:T(8,128)(2,1)S(1)}, u32[]{:S(2)}, u32[]{:S(2)}) collective-permute-start(bf16[6,40]{1,0:T(8,128)(2,1)S(1)} %get-tuple-element.480), channel_id=1, source_target_pairs={{480,0},{0,32},{32,64},{64,96},{96,128},{128,160},{160,192},{192,2... | collective-permute-start | bytes 1448 | tf_op jit(solution)/shard_map/while/body/eval_jaxpr/ppermute | solution.py:17
  326.3 13.2 %collective-permute-start.2 = (bf16[6,40]{1,0:T(8,128)(2,1)S(1)}, bf16[6,40]{1,0:T(8,128)(2,1)S(1)}, u32[]{:S(2)}, u32[]{:S(2)}) collective-permute-start(bf16[6,40]{1,0:T(8,128)(2,1)S(1)} %get-tuple-element.479), channel_id=1, source_target_pairs={{480,0},{0,32},{32,64},{64,96},{96,128},{128,160},{160,192},{192,2... | collective-permute-start | bytes 1448 | tf_op jit(solution)/shard_map/while/body/eval_jaxpr/ppermute | solution.py:17
  341.2 24.2 %collective-permute-start = (bf16[6,5120]{1,0:T(8,128)(2,1)S(1)}, bf16[6,5120]{1,0:T(8,128)(2,1)S(1)}, u32[]{:S(2)}, u32[]{:S(2)}) collective-permute-start(bf16[6,5120]{1,0:T(8,128)(2,1)S(1)} %get-tuple-element.478), channel_id=1, source_target_pairs={{480,0},{0,32},{32,64},{64,96},{96,128},{128,160},{160,192},{192,2... | collective-permute-start | bytes 184328 | tf_op jit(solution)/shard_map/while/body/eval_jaxpr/ppermute | solution.py:17
  347.9 18.7 %collective-permute-start.1 = (bf16[6,40]{1,0:T(8,128)(2,1)S(1)}, bf16[6,40]{1,0:T(8,128)(2,1)S(1)}, u32[]{:S(2)}, u32[]{:S(2)}) collective-permute-start(bf16[6,40]{1,0:T(8,128)(2,1)S(1)} %get-tuple-element.480), channel_id=1, source_target_pairs={{480,0},{0,32},{32,64},{64,96},{96,128},{128,160},{160,192},{192,2... | collective-permute-start | bytes 1448 | tf_op jit(solution)/shard_map/while/body/eval_jaxpr/ppermute | solution.py:17
  350.8 15.8 %collective-permute-start.2 = (bf16[6,40]{1,0:T(8,128)(2,1)S(1)}, bf16[6,40]{1,0:T(8,128)(2,1)S(1)}, u32[]{:S(2)}, u32[]{:S(2)}) collective-permute-start(bf16[6,40]{1,0:T(8,128)(2,1)S(1)} %get-tuple-element.479), channel_id=1, source_target_pairs={{480,0},{0,32},{32,64},{64,96},{96,128},{128,160},{160,192},{192,2... | collective-permute-start | bytes 1448 | tf_op jit(solution)/shard_map/while/body/eval_jaxpr/ppermute | solution.py:17
  368.6 19.7 %collective-permute-start = (bf16[6,5120]{1,0:T(8,128)(2,1)S(1)}, bf16[6,5120]{1,0:T(8,128)(2,1)S(1)}, u32[]{:S(2)}, u32[]{:S(2)}) collective-permute-start(bf16[6,5120]{1,0:T(8,128)(2,1)S(1)} %get-tuple-element.478), channel_id=1, source_target_pairs={{480,0},{0,32},{32,64},{64,96},{96,128},{128,160},{160,192},{192,2... | collective-permute-start | bytes 184328 | tf_op jit(solution)/shard_map/while/body/eval_jaxpr/ppermute | solution.py:17
  375.6 13.9 %collective-permute-start.1 = (bf16[6,40]{1,0:T(8,128)(2,1)S(1)}, bf16[6,40]{1,0:T(8,128)(2,1)S(1)}, u32[]{:S(2)}, u32[]{:S(2)}) collective-permute-start(bf16[6,40]{1,0:T(8,128)(2,1)S(1)} %get-tuple-element.480), channel_id=1, source_target_pairs={{480,0},{0,32},{32,64},{64,96},{96,128},{128,160},{160,192},{192,2... | collective-permute-start | bytes 1448 | tf_op jit(solution)/shard_map/while/body/eval_jaxpr/ppermute | solution.py:17
  392.8 22.4 %collective-permute-start = (bf16[6,5120]{1,0:T(8,128)(2,1)S(1)}, bf16[6,5120]{1,0:T(8,128)(2,1)S(1)}, u32[]{:S(2)}, u32[]{:S(2)}) collective-permute-start(bf16[6,5120]{1,0:T(8,128)(2,1)S(1)} %get-tuple-element.478), channel_id=1, source_target_pairs={{480,0},{0,32},{32,64},{64,96},{96,128},{128,160},{160,192},{192,2... | collective-permute-start | bytes 184328 | tf_op jit(solution)/shard_map/while/body/eval_jaxpr/ppermute | solution.py:17
  397.6 18.8 %collective-permute-start.1 = (bf16[6,40]{1,0:T(8,128)(2,1)S(1)}, bf16[6,40]{1,0:T(8,128)(2,1)S(1)}, u32[]{:S(2)}, u32[]{:S(2)}) collective-permute-start(bf16[6,40]{1,0:T(8,128)(2,1)S(1)} %get-tuple-element.480), channel_id=1, source_target_pairs={{480,0},{0,32},{32,64},{64,96},{96,128},{128,160},{160,192},{192,2... | collective-permute-start | bytes 1448 | tf_op jit(solution)/shard_map/while/body/eval_jaxpr/ppermute | solution.py:17
  401.9 14.5 %collective-permute-start.2 = (bf16[6,40]{1,0:T(8,128)(2,1)S(1)}, bf16[6,40]{1,0:T(8,128)(2,1)S(1)}, u32[]{:S(2)}, u32[]{:S(2)}) collective-permute-start(bf16[6,40]{1,0:T(8,128)(2,1)S(1)} %get-tuple-element.479), channel_id=1, source_target_pairs={{480,0},{0,32},{32,64},{64,96},{96,128},{128,160},{160,192},{192,2... | collective-permute-start | bytes 1448 | tf_op jit(solution)/shard_map/while/body/eval_jaxpr/ppermute | solution.py:17
  680.8 121.9 %all-to-all-start.1 = ((bf16[32,12,5120]{2,1,0:T(8,128)(2,1)}), bf16[32,12,5120]{2,1,0:T(8,128)(2,1)}, u32[]{:S(2)}, u32[]{:S(2)}) async-start(bf16[32,12,5120]{2,1,0:T(8,128)(2,1)} %reshape.205), calls=%async_computation.1 | async-start | bytes 10485760 | tf_op jit(solution)/shard_map/all_to_all | solution.py:153
  887.2 37.8 %collective-permute-start.6 = (bf16[8,5120]{1,0:T(8,128)(2,1)S(1)}, bf16[8,5120]{1,0:T(8,128)(2,1)S(1)}, u32[]{:S(2)}, u32[]{:S(2)}) collective-permute-start(bf16[8,5120]{1,0:T(8,128)(2,1)S(1)} %fusion.6), channel_id=1, source_target_pairs={{0,32},{32,64},{64,96},{96,128},{128,160},{160,192},{192,224},{224... | collective-permute-start | bytes 245768
  896.1 28.9 %collective-permute-start.7 = (bf16[8,5120]{1,0:T(8,128)(2,1)S(1)}, bf16[8,5120]{1,0:T(8,128)(2,1)S(1)}, u32[]{:S(2)}, u32[]{:S(2)}) collective-permute-start(bf16[8,5120]{1,0:T(8,128)(2,1)S(1)} %fusion.6), channel_id=1, source_target_pairs={{0,64},{32,96},{64,128},{96,160},{128,192},{160,224},{192,256},{22... | collective-permute-start | bytes 245768
  906.1 18.9 %collective-permute-start.8 = (bf16[8,5120]{1,0:T(8,128)(2,1)S(1)}, bf16[8,5120]{1,0:T(8,128)(2,1)S(1)}, u32[]{:S(2)}, u32[]{:S(2)}) collective-permute-start(bf16[8,5120]{1,0:T(8,128)(2,1)S(1)} %fusion.6), channel_id=1, source_target_pairs={{0,96},{32,128},{64,160},{96,192},{128,224},{160,256},{192,288},{2... | collective-permute-start | bytes 245768
  (32 other events, 2591.7 us)
where the time goes:
time: 929 us; the launch traced here: 927 us
  starting transfers between devices  374 us (40%)
  blocking collectives  281 us (30%)
  waiting for transfers between devices  170 us (18%)
  local copies, waits for them, and re-layouts  46.2 us (5%)
  matrix products  25.8 us (3%)
  other arithmetic  25.1 us (3%)
    ppermute x62, starting transfers between devices, from_behind(): return lax.ppermute(block, axis, route)  336 us
    all_to_all x1, blocking collectives, body(): lax.all_to_all(outgoing, 'ep', split_axis=0, concat_axis=0, tiled=True)  142 us
    all_to_all x1, waiting for transfers between devices, body(): lax.all_to_all(products.reshape(token_rows.shape), 'ep', split_axis=0, co...  116 us
    unnamed x1, blocking collectives  73.6 us
    all_gather x1, blocking collectives, body(): request_rows = lax.all_gather(expert_in, 'ctx', axis=0, tiled=True)  65.6 us
    ppermute x62, waiting for transfers between devices, from_behind(): return lax.ppermute(block, axis, route)  50.9 us
    unnamed x4, starting transfers between devices  32.4 us
  transfers between devices with their start and end apart: 67, of which 17 were waited for; matrix products, arithmetic and copies ran while one was open for 4% of the time, Pallas kernels for 0%

commit v1 on v0

v1 whole, which is shorter than its diff:
```python
import jax
import jax.numpy as jnp
from jax import lax
from jax.experimental import pallas as pl
from jax.experimental.pallas import tpu as pltpu
from jax.sharding import PartitionSpec as P

MESH = pl.DeviceIdType.MESH
BF16 = jnp.bfloat16
F32 = jnp.float32

GROUPS = 8
PER_GROUP = 5
HEAD = 128
TOK = 6
WIDTH = 5120
CACHE = 256
KEYS = 384
NY = 8
PART = 640
QUART = 1280
NEG = -1e30
FLOOR = -1e29

Q_AG = 0
Q_RS = 17
X_AG = 25
GO = 42
SIB_X = 62
SIB_P = 66
BACK = 70
Y_RS = 90
N_SEM = 98
CLASSES = (0, 1, -1, 2)


def iota(shape, dim):
    return lax.broadcasted_iota(jnp.int32, shape, dim)


def item_of(index, third):
    rho = index & 15
    late = rho - 12 + 4 * third
    tok = jnp.where(rho < 6, rho, jnp.where(rho < 12, rho - 6, jnp.where(late < 6, late, late - 6)))
    eighth = jnp.where(
        rho < 6, 2 * third, jnp.where(rho < 12, 2 * third + 1, jnp.where(late < 6, 6, 7))
    )
    return (index >> 4) * TOK + tok, eighth


def slot_of(index, third, half):
    rho = index & 15
    slot = jnp.where(rho < 12, rho, rho - 12 + 4 * third)
    eighth = jnp.where(rho < 12, 2 * third + half, 6 + half)
    return (index >> 4) * 16 + slot, eighth


def thirds_for(third, half):
    return sorted({third, half, half + 1})


def kernel(
    q_ref,
    new_ref,
    cache_ref,
    len_ref,
    res_ref,
    gain_ref,
    logit_ref,
    rid_ref,
    wg_ref,
    wu_ref,
    wd_ref,
    out_ref,
    qf,
    qg,
    pw,
    rin,
    za,
    zo,
    zi,
    attf,
    hid,
    xrow,
    xf,
    xg,
    sb,
    rb,
    po,
    ps,
    qb,
    rtn,
    rsb,
    rsi,
    zo2,
    zi2,
    wgu,
    wdx,
    kx,
    vx,
    newf,
    bias,
    send,
    recv,
    local,
):
    ctx = lax.axis_index("ctx")
    ep = lax.axis_index("ep")
    y, zh = lax.div(ctx, 2), lax.rem(ctx, 2)
    zl, x, core = lax.div(ep, 8), lax.rem(lax.div(ep, 2), 4), lax.rem(ep, 2)
    z = zh * 4 + zl
    expert = zl * 4 + x

    def at(dy=0, dz=0, dx=0, flip=False):
        ny = lax.rem(y + dy + NY, NY)
        nz = lax.rem(z + dz + 8, 8)
        nx = lax.rem(x + dx + 4, 4)
        nc = 1 - core if flip else core
        return (ny * 2 + lax.div(nz, 4), lax.rem(nz, 4) * 8 + nx * 2 + nc)

    def remote(src, dst, sem, device):
        return pltpu.make_async_remote_copy(
            src_ref=src,
            dst_ref=dst,
            send_sem=send.at[sem],
            recv_sem=recv.at[sem],
            device_id=device,
            device_id_type=MESH,
        )

    copies = [
        pltpu.make_async_copy(wg_ref.at[0], wgu.at[:, 0:128], local.at[0]),
        pltpu.make_async_copy(wu_ref.at[0], wgu.at[:, 128:256], local.at[1]),
    ]
    for j in range(3):
        copies.append(
            pltpu.make_async_copy(
                wd_ref.at[0, :, j * QUART : (j + 1) * QUART], wdx.at[j, 0:128], local.at[2 + 2 * j]
            )
        )
        copies.append(
            pltpu.make_async_copy(
                wd_ref.at[0, :, 3 * QUART : 4 * QUART], wdx.at[j, 128:256], local.at[3 + 2 * j]
            )
        )
    cache_copies = []
    for g in range(GROUPS):
        cols = slice(g * HEAD, (g + 1) * HEAD)
        cache_copies.append(
            pltpu.make_async_copy(
                cache_ref.at[0, 0, :, cols], kx.at[g, 0:CACHE], local.at[8 + 2 * g]
            )
        )
        cache_copies.append(
            pltpu.make_async_copy(
                cache_ref.at[1, 0, :, cols], vx.at[g, 0:CACHE, 0:HEAD], local.at[9 + 2 * g]
            )
        )
    for copy in cache_copies + copies:
        copy.start()

    barrier = pltpu.get_barrier_semaphore()
    partners = [at(dy=d) for d in range(1, NY)] + [at(dz=4), at(flip=True)]
    for dz in (0, 1, -1, 2, -2):
        partners += [at(dz=dz, dx=dx) for dx in range(4) if (dz, dx) != (0, 0)]
    for device in partners:
        pl.semaphore_signal(barrier, inc=1, device_id=device, device_id_type=MESH)

    qf[...] = jnp.zeros_like(qf)
    queries = q_ref[0].astype(F32)
    for g in range(GROUPS):
        for j in range(PER_GROUP):
            h = g * PER_GROUP + j
            qf[g, j * TOK : (j + 1) * TOK, :] = queries[:, h * HEAD : (h + 1) * HEAD]
    qg[ctx] = qf[...].astype(BF16)

    pl.semaphore_wait(barrier, len(partners))

    def block_of(dy, a):
        return lax.rem(y + dy + NY, NY) * 2 + (zh if a == 0 else 1 - zh)

    def gather(buf, base, on_step):
        started = []
        links = {}

        def link(way, d, a):
            if (way, d, a) not in links:
                sign = 1 if way == 0 else -1
                block = buf.at[block_of(-sign * (d - 1), a)]
                links[way, d, a] = remote(
                    block, block, base + 1 + (way * 4 + d - 1) * 2 + a, at(dy=sign)
                )
            return links[way, d, a]

        def go(way, d, a):
            link(way, d, a).start()
            started.append(link(way, d, a))

        own = buf.at[ctx]
        across = remote(own, own, base, at(dz=4))
        across.start()
        go(0, 1, 0)
        go(1, 1, 0)
        across.wait_recv()
        go(0, 1, 1)
        go(1, 1, 1)
        on_step(0)
        for d in range(1, 5):
            for a in (0, 1):
                for way in (0, 1):
                    if d == 4 and way != a:
                        continue
                    link(way, d, a).wait_recv()
                    if d < 3 or (d == 3 and way == a):
                        go(way, d + 1, a)
            on_step(d)
        across.wait_send()
        for copy in started:
            copy.wait_send()

    newf[...] = jnp.zeros_like(newf)
    newf[0, 0:TOK, :] = new_ref[0, 0].astype(F32)
    newf[1, 0:TOK, :] = new_ref[1, 0].astype(F32)
    for g in range(GROUPS):
        cols = slice(g * HEAD, (g + 1) * HEAD)
        kx[g, CACHE : CACHE + 16, :] = newf[0, :, cols].astype(BF16)
        vx[g, CACHE : CACHE + 16, 0:HEAD] = newf[1, :, cols].astype(BF16)
        kx[g, CACHE + 16 : KEYS, :] = jnp.zeros((KEYS - CACHE - 16, HEAD), BF16)
        vx[g, CACHE + 16 : KEYS, 0:HEAD] = jnp.zeros((KEYS - CACHE - 16, HEAD), BF16)
        vx[g, :, HEAD : 2 * HEAD] = jnp.ones((KEYS, HEAD), BF16)

    ids = rid_ref[...]
    one_hot = (ids == iota((96, 128), 1)).astype(F32)
    before = (iota((96, 96), 1) < iota((96, 96), 0)).astype(BF16)
    counts = jnp.dot(before, one_hot.astype(BF16), preferred_element_type=F32)
    rank = jnp.sum(counts * one_hot, axis=1, keepdims=True)
    slot_col = ids.astype(F32) * 16.0 + rank
    slot_lane = jnp.sum(
        jnp.where(iota((96, 128), 0) == iota((96, 128), 1), slot_col, 0.0), axis=0, keepdims=True
    )

    for copy in cache_copies:
        copy.wait()

    limit = jnp.minimum(len_ref[0] - ctx * CACHE, CACHE)
    scale = HEAD ** (-0.5)

    def attend(blocks):
        count = len(blocks)
        rows = 32 * count
        row = iota((rows, KEYS), 0)
        lane = iota((rows, KEYS), 1)
        r = row & 31
        tok = r
        for edge in (6, 12, 18, 24):
            tok = tok - jnp.where(r >= edge, 6, 0)
        for i, block in enumerate(blocks):
            tok = tok + jnp.where((row >> 5) == i, block * TOK, 0)
        new_ok = (lane >= CACHE) & (lane < CACHE + TOK) & (ctx * TOK + lane - CACHE <= tok)
        bias[0:rows, :] = jnp.where((lane < limit) | new_ok, 0.0, NEG)

        def group(g, carry):
            q = jnp.concatenate([qg[block, g] for block in blocks], axis=0)
            scores = lax.dot_general(
                q, kx[g], (((1,), (1,)), ((), ())), preferred_element_type=F32
            )
            scores = scores * scale + bias[0:rows, :]
            top = jnp.maximum(jnp.max(scores, axis=1, keepdims=True), FLOOR)
            top = top.astype(BF16).astype(F32)
            weights = jnp.exp(scores - top).astype(BF16)
            sums = jnp.dot(weights, vx[g], preferred_element_type=F32)
            shape = (count, 32, HEAD)
            weighted = sums[:, 0:HEAD].reshape(shape)
            total = sums[:, HEAD : 2 * HEAD].reshape(shape)
            tops = jnp.broadcast_to(top, (rows, HEAD)).reshape(shape)
            on = (iota(shape, 2) & 31) == iota(shape, 1)
            top_row = jnp.sum(jnp.where(on, tops, 0.0), axis=1, keepdims=True)
            total_row = jnp.sum(jnp.where(on, total, 0.0), axis=1, keepdims=True)
            at_row = iota(shape, 1)
            packed = jnp.where(
                at_row == 30, top_row, jnp.where(at_row == 31, total_row, weighted)
            ).astype(BF16)
            for i, block in enumerate(blocks):
                pw[block, g] = packed[i]
            return carry

        lax.fori_loop(0, GROUPS, group, 0)

    scatters = []

    def pair_of(dy):
        return pl.ds(lax.rem(y + dy + NY, NY) * 2, 2)

    def scatter(src, dst, base, d):
        copy = remote(src.at[pair_of(d)], dst.at[y], base + (d + NY) % NY - 1, at(dy=d))
        copy.start()
        scatters.append(copy)

    def attend_step(d):
        if d == 0:
            attend([block_of(0, 0), block_of(0, 1)])
            rin[y] = pw[pair_of(0)]
        elif d == 4:
            attend([block_of(4, 0), block_of(4, 1)])
            scatter(pw, rin, Q_RS, 4)
        else:
            attend([block_of(-d, 0), block_of(-d, 1), block_of(d, 0), block_of(d, 1)])
            scatter(pw, rin, Q_RS, -d)
            scatter(pw, rin, Q_RS, d)

    gather(qg, Q_AG, attend_step)
    for copy in scatters:
        copy.wait()
    scatters.clear()

    def merge(stack, count, normalize):
        wide = stack.astype(F32)
        tops = wide[:, 30, :]
        totals = wide[:, 31, :]
        top = jnp.max(tops, axis=0, keepdims=True)
        factor = jnp.exp(tops - top)
        total = jnp.sum(factor * totals, axis=0, keepdims=True)
        if normalize:
            factor = factor / total
        lane = iota((32, 128), 1)
        row = iota((32, 128), 0)
        on = ((lane & 31) == row) & (row < 30)
        merged = jnp.zeros((32, HEAD), F32)
        for part in range(count // 4):
            spread = jnp.zeros((32, 128), F32)
            for i in range(4):
                spread = jnp.where((lane >> 5) == i, factor[4 * part + i : 4 * part + i + 1], spread)
            spread = jnp.where(on, spread, 0.0)
            high = spread.astype(BF16)
            low = (spread - high.astype(F32)).astype(BF16)
            rows = stack[4 * part : 4 * part + 4].reshape(128, HEAD)
            merged = merged + jnp.dot(high, rows, preferred_element_type=F32)
            merged = merged + jnp.dot(low, rows, preferred_element_type=F32)
        return merged, top, total

    def merge_y(block, dst):
        def group(g, carry):
            merged, top, total = merge(rin[:, block, g], NY, False)
            at_row = iota((32, HEAD), 0)
            dst[g] = jnp.where(
                at_row == 30, top, jnp.where(at_row == 31, total, merged)
            ).astype(BF16)
            return carry

        lax.fori_loop(0, GROUPS, group, 0)

    merge_y(1 - zh, zo)
    across = remote(zo, zi, Q_RS + 7, at(dz=4))
    across.start()
    merge_y(zh, za)
    across.wait()

    def merge_z(g, carry):
        own, other = za[g], zi[g]
        empty_row = iota((2, 32, HEAD), 1)
        empty = jnp.where(empty_row == 30, FLOOR, 0.0).astype(BF16)
        stack = jnp.concatenate([own[None], other[None], empty], axis=0)
        merged, _, _ = merge(stack, 4, True)
        attf[g] = merged
        return carry

    lax.fori_loop(0, GROUPS, merge_z, 0)

    for g in range(GROUPS):
        for j in range(PER_GROUP):
            h = g * PER_GROUP + j
            cols = slice(h * HEAD, (h + 1) * HEAD)
            state = res_ref[0, :, cols].astype(F32) + attf[g, j * TOK : (j + 1) * TOK, :]
            hid[0:TOK, cols] = state.astype(BF16).astype(F32)
    state = hid[0:TOK, :]
    inv_rms = lax.rsqrt(jnp.mean(state * state, axis=1, keepdims=True) + 1e-05)
    logit = jnp.broadcast_to(logit_ref[...], (TOK, TOK))
    logit = jnp.sum(
        jnp.where(iota((TOK, TOK), 0) == iota((TOK, TOK), 1), logit, 0.0), axis=1, keepdims=True
    )
    gate = 1.0 / (1.0 + jnp.exp(-logit))
    xrow[0:TOK, :] = state * inv_rms * gain_ref[...].astype(F32) * gate

    def pieces():
        for e in range(6):
            yield (e % 2 * 6, e // 2 * PART), (0, e * PART), 6
        yield (12, 0), (0, 6 * PART), 4
        yield (12, PART), (4, 6 * PART), 2
        yield (14, PART), (0, 7 * PART), 2
        yield (12, 2 * PART), (2, 7 * PART), 4

    for (pr, pc), (wr, wc), n in pieces():
        xf[pr : pr + n, pc : pc + PART] = xrow[wr : wr + n, wc : wc + PART]
    xg[ctx] = xf[...].astype(BF16)

    gather(xg, X_AG, lambda d: None)

    rows_in = [xg[:, :, k * PART : (k + 1) * PART].reshape(256, PART) for k in range(3)]
    lanes = iota((96, 256), 1)
    lane_slots = []
    for k in range(3):
        tok, _ = item_of(lanes, k)
        lane_slots.append(
            jnp.sum(jnp.where(iota((96, 256), 0) == tok, slot_col, 0.0), axis=0, keepdims=True)
        )
    for j in range(3):
        for half in range(2):
            target, eighth_row = slot_of(iota((256, 256), 0), j, half)
            target = target.astype(F32)
            total = jnp.zeros((256, PART), F32)
            for k in thirds_for(j, half):
                _, eighth_lane = item_of(iota((256, 256), 1), k)
                pick = (lane_slots[k] == target) & (eighth_lane == eighth_row)
                pick = jnp.where(pick, 1.0, 0.0).astype(BF16)
                total = total + jnp.dot(pick, rows_in[k], preferred_element_type=F32)
            start = j * QUART + half * PART
            sb[:, :, start : start + PART] = total.astype(BF16).reshape(16, 16, PART)

    own_block = pltpu.make_async_copy(sb.at[expert], rb.at[core, 0], local.at[24])
    own_block.start()
    HALF = 3 * QUART // 2

    def routes(cls):
        for dx in range(4):
            if cls == 3:
                yield 12 + dx, slice(0, HALF), 2, dx, 12 + 2 * dx
                yield 12 + dx, slice(HALF, 2 * HALF), -2, dx, 13 + 2 * dx
            elif (cls, dx) != (0, 0):
                yield cls * 4 + dx, slice(0, 2 * HALF), CLASSES[cls], dx, cls * 4 + dx

    sent = [[], [], [], []]
    for cls in (3, 1, 2, 0):
        for i, cols, dz, dx, sem in routes(cls):
            to = lax.rem(zl + dz + 4, 4) * 4 + lax.rem(x + dx, 4)
            copy = remote(
                sb.at[to, :, cols], rb.at[core, i, :, cols], GO + sem, at(dz=dz, dx=dx)
            )
            copy.start()
            sent[cls].append(copy)

    for copy in copies:
        copy.wait()

    def experts(rows):
        n = rows.shape[0]
        main = jnp.dot(rows, wgu[0 : 3 * QUART, :], preferred_element_type=F32)
        r = iota((n, 256), 0) & 15
        tail = None
        for j in (2, 1, 0):
            part = jnp.dot(
                rows[:, j * QUART : (j + 1) * QUART],
                wgu[3 * QUART : 4 * QUART, :],
                preferred_element_type=F32,
            )
            part = pltpu.roll(part, n - 12 + 4 * j, 0)
            tail = part if tail is None else jnp.where(r < 4 * (j + 1), part, tail)
        both = main + tail
        gate_out, up_out = both[:, 0:128], both[:, 128:256]
        act = gate_out / (1.0 + jnp.exp(-gate_out)) * up_out
        r = iota((n, 128), 0) & 15
        act = jnp.where(r < 12, act, 0.0).astype(BF16).astype(F32)
        results = []
        for j in range(3):
            late = jnp.where(r >= 12, pltpu.roll(act, 12 - 4 * j, 0), 0.0)
            left = jnp.concatenate([act, late], axis=1).astype(BF16)
            results.append(jnp.dot(left, wdx[j], preferred_element_type=F32).astype(BF16))
        return results

    def run_experts(src, dst):
        rows = src.reshape(64, 3 * QUART)
        for j, part in enumerate(experts(rows)):
            dst[:, :, j * QUART : (j + 1) * QUART] = part.reshape(4, 16, QUART)

    across_x = []
    for cls in range(4):
        for copy in sent[cls]:
            copy.wait_recv()
        if cls == 0:
            own_block.wait()
        blocks = rb.at[core, pl.ds(cls * 4, 4)]
        copy = remote(blocks, blocks, SIB_X + cls, at(flip=True))
        copy.start()
        across_x.append(copy)
        run_experts(rb[core, cls * 4 : cls * 4 + 4], po.at[cls * 4 : cls * 4 + 4])

    across_p = []
    for cls in range(4):
        across_x[cls].wait_recv()
        run_experts(rb[1 - core, cls * 4 : cls * 4 + 4], ps.at[cls * 4 : cls * 4 + 4])
        blocks = pl.ds(cls * 4, 4)
        copy = remote(ps.at[blocks], qb.at[blocks], SIB_P + cls, at(flip=True))
        copy.start()
        across_p.append(copy)

    back = []
    for cls in range(4):
        across_p[cls].wait_recv()
        blocks = slice(cls * 4, cls * 4 + 4)
        po[blocks] = (po[blocks].astype(F32) + qb[blocks].astype(F32)).astype(BF16)
        for i, cols, dz, dx, sem in routes(cls):
            copy = remote(
                po.at[i, :, cols], rtn.at[expert, :, cols], BACK + sem, at(dz=-dz, dx=-dx)
            )
            copy.start()
            back.append(copy)
        if cls == 0:
            own_back = pltpu.make_async_copy(po.at[0], rtn.at[expert], local.at[25])
            own_back.start()

    for cls in range(4):
        for copy in sent[cls]:
            copy.wait_send()
        across_x[cls].wait_send()
        across_p[cls].wait_send()
    own_back.wait()
    for copy in back:
        copy.wait()

    lanes = iota((256, 128), 1)
    for k in range(3):
        tok, _ = item_of(iota((256, 128), 0), k)
        row_slots = jnp.sum(jnp.where(lanes == tok, slot_lane, 0.0), axis=1, keepdims=True)
        _, eighth_row = item_of(iota((256, 256), 0), k)
        total = jnp.zeros((256, PART), F32)
        for j in range(3):
            for half in range(2):
                if k not in thirds_for(j, half):
                    continue
                target, eighth_lane = slot_of(iota((256, 256), 1), j, half)
                pick = (row_slots == target.astype(F32)) & (eighth_lane == eighth_row)
                pick = jnp.where(pick, 1.0, 0.0).astype(BF16)
                start = j * QUART + half * PART
                source = rtn[:, :, start : start + PART].reshape(256, PART)
                total = total + jnp.dot(pick, source, preferred_element_type=F32)
        rsb[:, :, k * PART : (k + 1) * PART] = total.astype(BF16).reshape(16, 16, PART)

    rsi[y] = rsb[pair_of(0)]
    for d in (4, 3, -3, 2, -2, 1, -1):
        scatter(rsb, rsi, Y_RS, d)
    for copy in scatters:
        copy.wait()

    def add_up(block):
        total = rsi[0, block].astype(F32)
        for i in range(1, NY):
            total = total + rsi[i, block].astype(F32)
        return total

    zo2[...] = add_up(1 - zh).astype(BF16)
    across = remote(zo2, zi2, Y_RS + 7, at(dz=4))
    across.start()
    xf[...] = add_up(zh)
    across.wait()
    xf[...] = xf[...] + zi2[...].astype(F32)
    for (pr, pc), (wr, wc), n in pieces():
        xrow[wr : wr + n, wc : wc + PART] = xf[pr : pr + n, pc : pc + PART]
    out_ref[0] = (hid[0:TOK, :] + xrow[0:TOK, :]).astype(BF16)


def body(
    queries,
    new_kv,
    cached_key_value,
    cache_len,
    residual,
    norm_gain,
    route_logit,
    route_id,
    w_gate,
    w_up,
    w_down,
):
    vmem = pl.BlockSpec(memory_space=pltpu.VMEM)
    smem = pl.BlockSpec(memory_space=pltpu.SMEM)
    hbm = pl.BlockSpec(memory_space=pl.ANY)
    block = (GROUPS, 32, HEAD)
    slots = (16, 16, 3 * QUART)
    return pl.pallas_call(
        kernel,
        out_shape=jax.ShapeDtypeStruct((1, TOK, WIDTH), BF16),
        in_specs=[vmem, vmem, hbm, smem, vmem, vmem, vmem, vmem, hbm, hbm, hbm],
        out_specs=vmem,
        scratch_shapes=[
            pltpu.VMEM(block, F32),
            pltpu.VMEM((16,) + block, BF16),
            pltpu.VMEM((16,) + block, BF16),
            pltpu.VMEM((NY, 2) + block, BF16),
            pltpu.VMEM(block, BF16),
            pltpu.VMEM(block, BF16),
            pltpu.VMEM(block, BF16),
            pltpu.VMEM(block, F32),
            pltpu.VMEM((8, WIDTH), F32),
            pltpu.VMEM((8, WIDTH), F32),
            pltpu.VMEM((16, 3 * PART), F32),
            pltpu.VMEM((16, 16, 3 * PART), BF16),
            pltpu.VMEM(slots, BF16),
            pltpu.VMEM((2,) + slots, BF16),
            pltpu.VMEM(slots, BF16),
            pltpu.VMEM(slots, BF16),
            pltpu.VMEM(slots, BF16),
            pltpu.VMEM(slots, BF16),
            pltpu.VMEM((16, 16, 3 * PART), BF16),
            pltpu.VMEM((NY, 2, 16, 3 * PART), BF16),
            pltpu.VMEM((16, 3 * PART), BF16),
            pltpu.VMEM((16, 3 * PART), BF16),
            pltpu.VMEM((WIDTH, 256), BF16),
            pltpu.VMEM((3, 256, QUART), BF16),
            pltpu.VMEM((GROUPS, KEYS, HEAD), BF16),
            pltpu.VMEM((GROUPS, KEYS, 2 * HEAD), BF16),
            pltpu.VMEM((2, 16, GROUPS * HEAD), F32),
            pltpu.VMEM((128, KEYS), F32),
            pltpu.SemaphoreType.DMA((N_SEM,)),
            pltpu.SemaphoreType.DMA((N_SEM,)),
            pltpu.SemaphoreType.DMA((26,)),
        ],
        compiler_params=pltpu.CompilerParams(
            collective_id=0, has_side_effects=True, vmem_limit_bytes=56 * 1024 * 1024
        ),
    )(
        queries,
        new_kv,
        cached_key_value,
        cache_len,
        residual,
        norm_gain.reshape(1, WIDTH),
        route_logit,
        route_id.reshape(96, 1),
        w_gate,
        w_up,
        w_down,
    )


def solution(mesh):
    placed = (
        P("ep", "ctx", None),
        P(None, "ep", "ctx", None),
        P(None, "ep", "ctx", None),
        P("ep"),
        P("ep", "ctx", None),
        P(),
        P("ep", "ctx"),
        P("ep", None, None),
        P("ep", None, "ctx"),
        P("ep", None, "ctx"),
        P("ep", "ctx", None),
    )
    return jax.shard_map(
        body, mesh=mesh, in_specs=placed, out_specs=P("ep", "ctx", None), check_vma=False
    )
```

time: 929 us -> 185 us (0.20)
  the two profiles are of different devices: /device:TPU:22 before, /device:TPU:16 now
where the time goes in v1:
time: 185 us
  Pallas kernels  178 us (96%)
  local copies, waits for them, and re-layouts  5.57 us (3%)
    pallas_call x1, Pallas kernels, body(): pl.pallas_call(kernel, out_shape=jax.ShapeDtypeStruct((1, TOK, WIDTH), BF...  178 us

profile of v1, /device:TPU:16, one launch (start us, length us, event | category | flops | bytes accessed | tf_op | source)
XLA Modules:
  0.0 184.6 jit_solution(3199216637487089392)
XLA Ops:
  0.7 1.3 reshape.6.gain_ref
  2.0 1.4 copy.12.new_ref
  3.3 1.4 copy.13.rid_ref
  4.7 178.4 %shard_map.109 = bf16[1,6,5120]{2,1,0:T(8,128)(2,1)} custom-call(bf16[1,6,5120]{2,1,0:T(8,128)(2,1)} %q_ref.1, bf16[2,1,6,1024]{3,2,1,0:T(8,128)(2,1)} %copy.12.new_ref, bf16[2,1,256,1024]{3,2,1,0:T(8,128)(2,1)} %cache_ref.1, s32[1]{0:T(128)S(6)} %copy.15.len_ref, bf16[1,6,5120]{2,1,0:T(8,128)(2,1)} %res_ref.1, bf16[1,5120]{1,0:T(2,128)(2,1)} %reshape.6.gain_ref, ...), custom_call_target="tpu_custom_call" | custom-call | tf_op jit(solution)/shard_map/pallas_call | solution.py:578
  183.1 1.5 copy.16

commit v2 on v1

--- a/solution.py
+++ b/solution.py
@@ -24,13 +24,13 @@
 
 Q_AG = 0
 Q_RS = 17
-X_AG = 25
-GO = 42
-SIB_X = 62
-SIB_P = 66
-BACK = 70
-Y_RS = 90
-N_SEM = 98
+X_AG = 28
+GO = 45
+SIB_X = 65
+SIB_P = 69
+BACK = 73
+Y_RS = 93
+N_SEM = 104
 CLASSES = (0, 1, -1, 2)
 
 
@@ -79,6 +79,9 @@
     za,
     zo,
     zi,
+    r3,
+    r4,
+    mg,
     attf,
     hid,
     xrow,
@@ -86,12 +89,14 @@
     xg,
     sb,
     rb,
-    po,
-    ps,
+    pp,
     qb,
     rtn,
     rsb,
     rsi,
+    f3,
+    f4,
+    fm,
     zo2,
     zi2,
     wgu,
@@ -160,7 +165,7 @@
         copy.start()
 
     barrier = pltpu.get_barrier_semaphore()
-    partners = [at(dy=d) for d in range(1, NY)] + [at(dz=4), at(flip=True)]
+    partners = [at(dy=d) for d in (1, -1, 2, -2)] + [at(dz=4), at(flip=True)]
     for dz in (0, 1, -1, 2, -2):
         partners += [at(dz=dz, dx=dx) for dx in range(4) if (dz, dx) != (0, 0)]
     for device in partners:
@@ -219,8 +224,9 @@
             copy.wait_send()
 
     newf[...] = jnp.zeros_like(newf)
-    newf[0, 0:TOK, :] = new_ref[0, 0].astype(F32)
-    newf[1, 0:TOK, :] = new_ref[1, 0].astype(F32)
+    fresh = new_ref[0].astype(F32)
+    newf[0, 0:TOK, :] = fresh[:, 0, :]
+    newf[1, 0:TOK, :] = fresh[:, 1, :]
     for g in range(GROUPS):
         cols = slice(g * HEAD, (g + 1) * HEAD)
         kx[g, CACHE : CACHE + 16, :] = newf[0, :, cols].astype(BF16)
@@ -229,7 +235,9 @@
         vx[g, CACHE + 16 : KEYS, 0:HEAD] = jnp.zeros((KEYS - CACHE - 16, HEAD), BF16)
         vx[g, :, HEAD : 2 * HEAD] = jnp.ones((KEYS, HEAD), BF16)
 
-    ids = rid_ref[...]
+    ids = jnp.sum(
+        jnp.where(iota((96, 96), 0) == iota((96, 96), 1), rid_ref[0], 0), axis=1, keepdims=True
+    )
     one_hot = (ids == iota((96, 128), 1)).astype(F32)
     before = (iota((96, 96), 1) < iota((96, 96), 0)).astype(BF16)
     counts = jnp.dot(before, one_hot.astype(BF16), preferred_element_type=F32)
@@ -291,27 +299,53 @@
     def pair_of(dy):
         return pl.ds(lax.rem(y + dy + NY, NY) * 2, 2)
 
-    def scatter(src, dst, base, d):
-        copy = remote(src.at[pair_of(d)], dst.at[y], base + (d + NY) % NY - 1, at(dy=d))
+    def ship(src, dst, sem, d):
+        copy = remote(src, dst, sem, at(dy=d))
         copy.start()
         scatters.append(copy)
+        return copy
+
+    def ship_near(src, dst, base):
+        ship(src.at[pair_of(1)], dst.at[1], base, 1)
+        ship(src.at[pair_of(-1)], dst.at[2], base + 1, -1)
+
+    def ship_three(src, dst, base):
+        up = ship(src.at[pair_of(3)], dst.at[0], base + 2, 1)
+        down = ship(src.at[pair_of(-3)], dst.at[1], base + 3, -1)
+        return up, down
+
+    def ship_four(src, dst, base):
+        up = ship(src.at[block_of(4, 0)], dst.at[0], base + 4, 2)
+        down = ship(src.at[block_of(4, 1)], dst.at[1], base + 5, -2)
+        return up, down
+
+    far = {}
 
     def attend_step(d):
         if d == 0:
             attend([block_of(0, 0), block_of(0, 1)])
-            rin[y] = pw[pair_of(0)]
+            rin[0] = pw[pair_of(0)]
         elif d == 4:
             attend([block_of(4, 0), block_of(4, 1)])
-            scatter(pw, rin, Q_RS, 4)
+            far[4] = ship_four(pw, r4, Q_RS)
         else:
             attend([block_of(-d, 0), block_of(-d, 1), block_of(d, 0), block_of(d, 1)])
-            scatter(pw, rin, Q_RS, -d)
-            scatter(pw, rin, Q_RS, d)
-
+            if d == 1:
+                ship_near(pw, rin, Q_RS)
+            if d == 3:
+                far[3] = ship_three(pw, r3, Q_RS)
+
+    empty_row = iota((3, 32, HEAD), 1)
+    empty = jnp.where(empty_row == 30, FLOOR, 0.0).astype(BF16)
+
+    def settle_rin(g, carry):
+        for i in range(3):
+            for a in range(2):
+                rin[5 + i, a, g] = empty[i]
+        return carry
+
+    lax.fori_loop(0, GROUPS, settle_rin, 0)
     gather(qg, Q_AG, attend_step)
-    for copy in scatters:
-        copy.wait()
-    scatters.clear()
 
     def merge(stack, count, normalize):
         wide = stack.astype(F32)
@@ -338,28 +372,54 @@
             merged = merged + jnp.dot(low, rows, preferred_element_type=F32)
         return merged, top, total
 
+    def merged_block(stack, count):
+        merged, top, total = merge(stack, count, False)
+        at_row = iota((32, HEAD), 0)
+        return jnp.where(at_row == 30, top, jnp.where(at_row == 31, total, merged)).astype(BF16)
+
+    for side in (0, 1):
+        far[3][side].wait_recv()
+        for a in (1 - side, side):
+            if a == side:
+                far[4][side].wait_recv()
+
+            def group(g, carry, side=side, a=a):
+                position = zh if a == 0 else 1 - zh
+                own = pw[block_of(2 - 4 * side, a), g]
+                third = r3[side, position, g]
+                fourth = r4[side, g] if a == side else empty[0]
+                stack = jnp.concatenate([own[None], third[None], fourth[None], empty[0:1]], axis=0)
+                mg[side, a, g] = merged_block(stack, 4)
+                return carry
+
+            lax.fori_loop(0, GROUPS, group, 0)
+            position = zh if a == 0 else 1 - zh
+            ship(
+                mg.at[side, a], rin.at[3 + side, position], Q_RS + 6 + 2 * side + a, 2 - 4 * side
+            )
+    for copy in scatters:
+        copy.wait_send()
+    for copy in scatters:
+        if not any(copy is other for other in far[3] + far[4]):
+            copy.wait_recv()
+    scatters.clear()
+
     def merge_y(block, dst):
         def group(g, carry):
-            merged, top, total = merge(rin[:, block, g], NY, False)
-            at_row = iota((32, HEAD), 0)
-            dst[g] = jnp.where(
-                at_row == 30, top, jnp.where(at_row == 31, total, merged)
-            ).astype(BF16)
+            dst[g] = merged_block(rin[:, block, g], NY)
             return carry
 
         lax.fori_loop(0, GROUPS, group, 0)
 
     merge_y(1 - zh, zo)
-    across = remote(zo, zi, Q_RS + 7, at(dz=4))
+    across = remote(zo, zi, Q_RS + 10, at(dz=4))
     across.start()
     merge_y(zh, za)
     across.wait()
 
     def merge_z(g, carry):
         own, other = za[g], zi[g]
-        empty_row = iota((2, 32, HEAD), 1)
-        empty = jnp.where(empty_row == 30, FLOOR, 0.0).astype(BF16)
-        stack = jnp.concatenate([own[None], other[None], empty], axis=0)
+        stack = jnp.concatenate([own[None], other[None], empty[0:2]], axis=0)
         merged, _, _ = merge(stack, 4, True)
         attf[g] = merged
         return carry
@@ -379,7 +439,7 @@
         jnp.where(iota((TOK, TOK), 0) == iota((TOK, TOK), 1), logit, 0.0), axis=1, keepdims=True
     )
     gate = 1.0 / (1.0 + jnp.exp(-logit))
-    xrow[0:TOK, :] = state * inv_rms * gain_ref[...].astype(F32) * gate
+    xrow[0:TOK, :] = state * inv_rms * gain_ref[...].reshape(1, WIDTH).astype(F32) * gate
 
     def pieces():
         for e in range(6):
@@ -416,24 +476,24 @@
             start = j * QUART + half * PART
             sb[:, :, start : start + PART] = total.astype(BF16).reshape(16, 16, PART)
 
-    own_block = pltpu.make_async_copy(sb.at[expert], rb.at[core, 0], local.at[24])
+    own_block = pltpu.make_async_copy(sb.at[expert], rb.at[0, core, 0], local.at[24])
     own_block.start()
     HALF = 3 * QUART // 2
 
     def routes(cls):
         for dx in range(4):
             if cls == 3:
-                yield 12 + dx, slice(0, HALF), 2, dx, 12 + 2 * dx
-                yield 12 + dx, slice(HALF, 2 * HALF), -2, dx, 13 + 2 * dx
+                yield slice(0, HALF), 2, dx, 12 + 2 * dx
+                yield slice(HALF, 2 * HALF), -2, dx, 13 + 2 * dx
             elif (cls, dx) != (0, 0):
-                yield cls * 4 + dx, slice(0, 2 * HALF), CLASSES[cls], dx, cls * 4 + dx
+                yield slice(0, 2 * HALF), CLASSES[cls], dx, cls * 4 + dx
 
     sent = [[], [], [], []]
-    for cls in (3, 1, 2, 0):
-        for i, cols, dz, dx, sem in routes(cls):
+    for cls in range(4):
+        for cols, dz, dx, sem in routes(cls):
             to = lax.rem(zl + dz + 4, 4) * 4 + lax.rem(x + dx, 4)
             copy = remote(
-                sb.at[to, :, cols], rb.at[core, i, :, cols], GO + sem, at(dz=dz, dx=dx)
+                sb.at[to, :, cols], rb.at[cls, core, dx, :, cols], GO + sem, at(dz=dz, dx=dx)
             )
             copy.start()
             sent[cls].append(copy)
@@ -466,46 +526,43 @@
             results.append(jnp.dot(left, wdx[j], preferred_element_type=F32).astype(BF16))
         return results
 
-    def run_experts(src, dst):
-        rows = src.reshape(64, 3 * QUART)
-        for j, part in enumerate(experts(rows)):
-            dst[:, :, j * QUART : (j + 1) * QUART] = part.reshape(4, 16, QUART)
-
+    back = []
     across_x = []
+    across_p = []
+
+    def send_back(cls):
+        across_p[cls].wait_recv()
+        pp[cls, core] = (pp[cls, core].astype(F32) + qb[cls].astype(F32)).astype(BF16)
+        for cols, dz, dx, sem in routes(cls):
+            copy = remote(
+                pp.at[cls, core, dx, :, cols],
+                rtn.at[expert, :, cols],
+                BACK + sem,
+                at(dz=-dz, dx=-dx),
+            )
+            copy.start()
+            back.append(copy)
+
     for cls in range(4):
         for copy in sent[cls]:
             copy.wait_recv()
         if cls == 0:
             own_block.wait()
-        blocks = rb.at[core, pl.ds(cls * 4, 4)]
+        blocks = rb.at[cls, core]
         copy = remote(blocks, blocks, SIB_X + cls, at(flip=True))
         copy.start()
         across_x.append(copy)
-        run_experts(rb[core, cls * 4 : cls * 4 + 4], po.at[cls * 4 : cls * 4 + 4])
-
-    across_p = []
-    for cls in range(4):
-        across_x[cls].wait_recv()
-        run_experts(rb[1 - core, cls * 4 : cls * 4 + 4], ps.at[cls * 4 : cls * 4 + 4])
-        blocks = pl.ds(cls * 4, 4)
-        copy = remote(ps.at[blocks], qb.at[blocks], SIB_P + cls, at(flip=True))
+        if cls > 0:
+            send_back(cls - 1)
+        copy.wait_recv()
+        for j, part in enumerate(experts(rb[cls].reshape(128, 3 * QUART))):
+            pp[cls, :, :, :, j * QUART : (j + 1) * QUART] = part.reshape(2, 4, 16, QUART)
+        copy = remote(pp.at[cls, 1 - core], qb.at[cls], SIB_P + cls, at(flip=True))
         copy.start()
         across_p.append(copy)
-
-    back = []
-    for cls in range(4):
-        across_p[cls].wait_recv()
-        blocks = slice(cls * 4, cls * 4 + 4)
-        po[blocks] = (po[blocks].astype(F32) + qb[blocks].astype(F32)).astype(BF16)
-        for i, cols, dz, dx, sem in routes(cls):
-            copy = remote(
-                po.at[i, :, cols], rtn.at[expert, :, cols], BACK + sem, at(dz=-dz, dx=-dx)
-            )
-            copy.start()
-            back.append(copy)
-        if cls == 0:
-            own_back = pltpu.make_async_copy(po.at[0], rtn.at[expert], local.at[25])
-            own_back.start()
+    send_back(3)
+    own_back = pltpu.make_async_copy(pp.at[0, core, 0], rtn.at[expert], local.at[25])
+    own_back.start()
 
     for cls in range(4):
         for copy in sent[cls]:
@@ -534,20 +591,36 @@
                 total = total + jnp.dot(pick, source, preferred_element_type=F32)
         rsb[:, :, k * PART : (k + 1) * PART] = total.astype(BF16).reshape(16, 16, PART)
 
-    rsi[y] = rsb[pair_of(0)]
-    for d in (4, 3, -3, 2, -2, 1, -1):
-        scatter(rsb, rsi, Y_RS, d)
+    far[3] = ship_three(rsb, f3, Y_RS)
+    far[4] = ship_four(rsb, f4, Y_RS)
+    ship_near(rsb, rsi, Y_RS)
+    rsi[0] = rsb[pair_of(0)]
+    for side in (0, 1):
+        far[3][side].wait_recv()
+        for a in (1 - side, side):
+            position = zh if a == 0 else 1 - zh
+            total = rsb[block_of(2 - 4 * side, a)].astype(F32) + f3[side, position].astype(F32)
+            if a == side:
+                far[4][side].wait_recv()
+                total = total + f4[side].astype(F32)
+            fm[side, a] = total.astype(BF16)
+            ship(
+                fm.at[side, a], rsi.at[3 + side, position], Y_RS + 6 + 2 * side + a, 2 - 4 * side
+            )
     for copy in scatters:
-        copy.wait()
+        copy.wait_send()
+    for copy in scatters:
+        if not any(copy is other for other in far[3] + far[4]):
+            copy.wait_recv()
 
     def add_up(block):
         total = rsi[0, block].astype(F32)
-        for i in range(1, NY):
+        for i in range(1, 5):
             total = total + rsi[i, block].astype(F32)
         return total
 
     zo2[...] = add_up(1 - zh).astype(BF16)
-    across = remote(zo2, zi2, Y_RS + 7, at(dz=4))
+    across = remote(zo2, zi2, Y_RS + 10, at(dz=4))
     across.start()
     xf[...] = add_up(zh)
     across.wait()
@@ -588,19 +661,24 @@
             pltpu.VMEM(block, BF16),
             pltpu.VMEM(block, BF16),
             pltpu.VMEM(block, BF16),
+            pltpu.VMEM((2, 2) + block, BF16),
+            pltpu.VMEM((2,) + block, BF16),
+            pltpu.VMEM((2, 2) + block, BF16),
             pltpu.VMEM(block, F32),
             pltpu.VMEM((8, WIDTH), F32),
             pltpu.VMEM((8, WIDTH), F32),
             pltpu.VMEM((16, 3 * PART), F32),
             pltpu.VMEM((16, 16, 3 * PART), BF16),
             pltpu.VMEM(slots, BF16),
-            pltpu.VMEM((2,) + slots, BF16),
-            pltpu.VMEM(slots, BF16),
-            pltpu.VMEM(slots, BF16),
-            pltpu.VMEM(slots, BF16),
+            pltpu.VMEM((4, 2, 4, 16, 3 * QUART), BF16),
+            pltpu.VMEM((4, 2, 4, 16, 3 * QUART), BF16),
+            pltpu.VMEM((4, 4, 16, 3 * QUART), BF16),
             pltpu.VMEM(slots, BF16),
             pltpu.VMEM((16, 16, 3 * PART), BF16),
-            pltpu.VMEM((NY, 2, 16, 3 * PART), BF16),
+            pltpu.VMEM((5, 2, 16, 3 * PART), BF16),
+            pltpu.VMEM((2, 2, 16, 3 * PART), BF16),
+            pltpu.VMEM((2, 16, 3 * PART), BF16),
+            pltpu.VMEM((2, 2, 16, 3 * PART), BF16),
             pltpu.VMEM((16, 3 * PART), BF16),
             pltpu.VMEM((16, 3 * PART), BF16),
             pltpu.VMEM((WIDTH, 256), BF16),
@@ -618,13 +696,13 @@
         ),
     )(
         queries,
-        new_kv,
+        jnp.transpose(new_kv, (1, 2, 0, 3)),
         cached_key_value,
         cache_len,
         residual,
-        norm_gain.reshape(1, WIDTH),
+        norm_gain,
         route_logit,
-        route_id.reshape(96, 1),
+        jnp.transpose(route_id, (0, 2, 1)),
         w_gate,
         w_up,
         w_down,

time: 185 us -> 169 us (0.914)
  the two profiles are of different devices: /device:TPU:16 before, /device:TPU:200 now
where the time goes in v2:
time: 169 us; the launch traced here: 168 us
  Pallas kernels  166 us (98%)
    pallas_call x1, Pallas kernels, body(): pl.pallas_call(kernel, out_shape=jax.ShapeDtypeStruct((1, TOK, WIDTH), BF...  166 us

profile of v2, /device:TPU:200, one launch (start us, length us, event | category | flops | bytes accessed | tf_op | source)
XLA Modules:
  0.0 168.5 jit_solution(16422936142203393823)
XLA Ops:
  0.7 166.3 %shard_map.109 = bf16[1,6,5120]{2,1,0:T(8,128)(2,1)} custom-call(bf16[1,6,5120]{2,1,0:T(8,128)(2,1)} %q_ref.1, bf16[1,6,2,1024]{3,2,1,0:T(2,128)(2,1)} %bitcast.2, bf16[2,1,256,1024]{3,2,1,0:T(8,128)(2,1)} %cache_ref.1, s32[1]{0:T(128)S(6)} %copy.13.len_ref, bf16[1,6,5120]{2,1,0:T(8,128)(2,1)} %res_ref.1, bf16[5120]{0:T(1024)(128)(2,1)} %gain_ref.1, ...), custom_call_target="tpu_custom_call" | custom-call | tf_op jit(solution)/shard_map/pallas_call | solution.py:651
  167.0 1.5 copy.14

commit v3 on v2

--- a/solution.py
+++ b/solution.py
@@ -23,14 +23,19 @@
 FLOOR = -1e29
 
 Q_AG = 0
-Q_RS = 17
-X_AG = 28
-GO = 45
-SIB_X = 65
-SIB_P = 69
-BACK = 73
-Y_RS = 93
-N_SEM = 104
+Z_RES = 18
+Q_RS = 20
+Q_Z = 30
+X_AG = 32
+GO = 48
+GO_Y = 57
+SIB_X = 63
+SIB_P = 67
+BACK_Y = 71
+BACK = 77
+Y_RS = 86
+Y_Z = 96
+N_SEM = 97
 CLASSES = (0, 1, -1, 2)
 
 
@@ -77,13 +82,17 @@
     pw,
     rin,
     za,
-    zo,
     zi,
     r3,
     r4,
     mg,
     attf,
+    rown,
+    rfar,
+    lown,
+    lfar,
     hid,
+    hid2,
     xrow,
     xf,
     xg,
@@ -91,6 +100,7 @@
     rb,
     pp,
     qb,
+    yq,
     rtn,
     rsb,
     rsi,
@@ -165,7 +175,7 @@
         copy.start()
 
     barrier = pltpu.get_barrier_semaphore()
-    partners = [at(dy=d) for d in (1, -1, 2, -2)] + [at(dz=4), at(flip=True)]
+    partners = [at(dy=d) for d in (1, -1, 2, -2)] + [at(dz=4), at(dy=4, dz=4), at(flip=True)]
     for dz in (0, 1, -1, 2, -2):
         partners += [at(dz=dz, dx=dx) for dx in range(4) if (dz, dx) != (0, 0)]
     for device in partners:
@@ -184,44 +194,69 @@
     def block_of(dy, a):
         return lax.rem(y + dy + NY, NY) * 2 + (zh if a == 0 else 1 - zh)
 
-    def gather(buf, base, on_step):
-        started = []
-        links = {}
-
-        def link(way, d, a):
-            if (way, d, a) not in links:
+    class Ring:
+        def __init__(self, buf, base):
+            self.buf, self.base, self.copies = buf, base, {}
+
+        def copy(self, way, d, a):
+            if (way, d, a) not in self.copies:
                 sign = 1 if way == 0 else -1
-                block = buf.at[block_of(-sign * (d - 1), a)]
-                links[way, d, a] = remote(
-                    block, block, base + 1 + (way * 4 + d - 1) * 2 + a, at(dy=sign)
-                )
-            return links[way, d, a]
-
-        def go(way, d, a):
-            link(way, d, a).start()
-            started.append(link(way, d, a))
-
-        own = buf.at[ctx]
-        across = remote(own, own, base, at(dz=4))
-        across.start()
-        go(0, 1, 0)
-        go(1, 1, 0)
-        across.wait_recv()
-        go(0, 1, 1)
-        go(1, 1, 1)
-        on_step(0)
-        for d in range(1, 5):
-            for a in (0, 1):
-                for way in (0, 1):
-                    if d == 4 and way != a:
-                        continue
-                    link(way, d, a).wait_recv()
-                    if d < 3 or (d == 3 and way == a):
-                        go(way, d + 1, a)
-            on_step(d)
-        across.wait_send()
-        for copy in started:
-            copy.wait_send()
+                block = self.buf.at[block_of(-sign * (d - 1), a)]
+                sem = self.base + (way * 4 + d - 1) * 2 + a
+                self.copies[way, d, a] = remote(block, block, sem, at(dy=sign))
+            return self.copies[way, d, a]
+
+        def go(self, d, a, ways=(0, 1)):
+            for way in ways:
+                self.copy(way, d, a).start()
+
+        def got(self, d, a, ways=(0, 1)):
+            for way in ways:
+                self.copy(way, d, a).wait_recv()
+
+        def pass_on(self, d, a, ways=(0, 1)):
+            for way in ways:
+                self.copy(way, d, a).wait_recv()
+                self.copy(way, d + 1, a).start()
+
+        def end(self):
+            for copy in self.copies.values():
+                copy.wait_send()
+
+    own = qg.at[ctx]
+    ring = Ring(qg, Q_AG + 2)
+    ring.go(1, 0)
+    near = remote(own, own, Q_AG, at(dz=4))
+    near.start()
+    opposite = remote(own, own, Q_AG + 1, at(dy=4, dz=4))
+    opposite.start()
+
+    def pieces():
+        for e in range(6):
+            yield (e % 2 * 6, e // 2 * PART), (0, e * PART), 6
+        yield (12, 0), (0, 6 * PART), 4
+        yield (12, PART), (4, 6 * PART), 2
+        yield (14, PART), (0, 7 * PART), 2
+        yield (12, 2 * PART), (2, 7 * PART), 4
+
+    def pack():
+        for (pr, pc), (wr, wc), n in pieces():
+            xf[pr : pr + n, pc : pc + PART] = xrow[wr : wr + n, wc : wc + PART]
+
+    def unpack():
+        for (pr, pc), (wr, wc), n in pieces():
+            xrow[wr : wr + n, wc : wc + PART] = xf[pr : pr + n, pc : pc + PART]
+
+    xrow[0:TOK, :] = res_ref[0].astype(F32)
+    pack()
+    rown[...] = xf[...].astype(BF16)
+    lown[...] = jnp.zeros_like(lown)
+    lown[0:1, 0:TOK] = logit_ref[...]
+    res_copy = remote(rown, rfar, Z_RES, at(dz=4))
+    res_copy.start()
+    logit_copy = remote(lown, lfar, Z_RES + 1, at(dz=4))
+    logit_copy.start()
+    rtn[...] = jnp.zeros_like(rtn)
 
     newf[...] = jnp.zeros_like(newf)
     fresh = new_ref[0].astype(F32)
@@ -292,7 +327,7 @@
                 pw[block, g] = packed[i]
             return carry
 
-        lax.fori_loop(0, GROUPS, group, 0)
+        lax.fori_loop(0, GROUPS, group, 0, unroll=2)
 
     scatters = []
 
@@ -321,20 +356,6 @@
 
     far = {}
 
-    def attend_step(d):
-        if d == 0:
-            attend([block_of(0, 0), block_of(0, 1)])
-            rin[0] = pw[pair_of(0)]
-        elif d == 4:
-            attend([block_of(4, 0), block_of(4, 1)])
-            far[4] = ship_four(pw, r4, Q_RS)
-        else:
-            attend([block_of(-d, 0), block_of(-d, 1), block_of(d, 0), block_of(d, 1)])
-            if d == 1:
-                ship_near(pw, rin, Q_RS)
-            if d == 3:
-                far[3] = ship_three(pw, r3, Q_RS)
-
     empty_row = iota((3, 32, HEAD), 1)
     empty = jnp.where(empty_row == 30, FLOOR, 0.0).astype(BF16)
 
@@ -345,7 +366,37 @@
         return carry
 
     lax.fori_loop(0, GROUPS, settle_rin, 0)
-    gather(qg, Q_AG, attend_step)
+    def both(d):
+        return [block_of(d, 0), block_of(d, 1)]
+
+    ring.pass_on(1, 0)
+    near.wait_recv()
+    ring.go(1, 1)
+    ring.pass_on(2, 0)
+    ring.pass_on(1, 1)
+    opposite.wait_recv()
+    beyond = []
+    for way, sign in ((0, 1), (1, -1)):
+        block = qg.at[block_of(4, 1)]
+        copy = remote(block, block, Q_AG + 2 + (way * 4 + 2) * 2 + 1, at(dy=sign))
+        copy.start()
+        beyond.append(copy)
+    attend(both(0) + both(-1) + both(1))
+    rin[0] = pw[pair_of(0)]
+    ship_near(pw, rin, Q_RS)
+    ring.pass_on(3, 0, (0,))
+    ring.got(3, 0, (1,))
+    ring.got(2, 1)
+    attend(both(-2) + both(2))
+    for copy in beyond:
+        copy.wait_recv()
+    ring.got(4, 0, (0,))
+    attend(both(-3) + both(3) + both(4))
+    far[3] = ship_three(pw, r3, Q_RS)
+    far[4] = ship_four(pw, r4, Q_RS)
+    ring.end()
+    for copy in beyond + [near, opposite, res_copy, logit_copy]:
+        copy.wait_send()
 
     def merge(stack, count, normalize):
         wide = stack.astype(F32)
@@ -404,56 +455,70 @@
             copy.wait_recv()
     scatters.clear()
 
-    def merge_y(block, dst):
+    def merge_y(block):
         def group(g, carry):
-            dst[g] = merged_block(rin[:, block, g], NY)
+            za[block, g] = merged_block(rin[:, block, g], NY)
             return carry
 
-        lax.fori_loop(0, GROUPS, group, 0)
-
-    merge_y(1 - zh, zo)
-    across = remote(zo, zi, Q_RS + 10, at(dz=4))
-    across.start()
-    merge_y(zh, za)
-    across.wait()
-
-    def merge_z(g, carry):
-        own, other = za[g], zi[g]
-        stack = jnp.concatenate([own[None], other[None], empty[0:2]], axis=0)
-        merged, _, _ = merge(stack, 4, True)
-        attf[g] = merged
-        return carry
-
-    lax.fori_loop(0, GROUPS, merge_z, 0)
-
-    for g in range(GROUPS):
-        for j in range(PER_GROUP):
-            h = g * PER_GROUP + j
-            cols = slice(h * HEAD, (h + 1) * HEAD)
-            state = res_ref[0, :, cols].astype(F32) + attf[g, j * TOK : (j + 1) * TOK, :]
-            hid[0:TOK, cols] = state.astype(BF16).astype(F32)
-    state = hid[0:TOK, :]
-    inv_rms = lax.rsqrt(jnp.mean(state * state, axis=1, keepdims=True) + 1e-05)
-    logit = jnp.broadcast_to(logit_ref[...], (TOK, TOK))
-    logit = jnp.sum(
-        jnp.where(iota((TOK, TOK), 0) == iota((TOK, TOK), 1), logit, 0.0), axis=1, keepdims=True
-    )
-    gate = 1.0 / (1.0 + jnp.exp(-logit))
-    xrow[0:TOK, :] = state * inv_rms * gain_ref[...].reshape(1, WIDTH).astype(F32) * gate
-
-    def pieces():
-        for e in range(6):
-            yield (e % 2 * 6, e // 2 * PART), (0, e * PART), 6
-        yield (12, 0), (0, 6 * PART), 4
-        yield (12, PART), (4, 6 * PART), 2
-        yield (14, PART), (0, 7 * PART), 2
-        yield (12, 2 * PART), (2, 7 * PART), 4
-
-    for (pr, pc), (wr, wc), n in pieces():
-        xf[pr : pr + n, pc : pc + PART] = xrow[wr : wr + n, wc : wc + PART]
-    xg[ctx] = xf[...].astype(BF16)
-
-    gather(xg, X_AG, lambda d: None)
+        lax.fori_loop(0, GROUPS, group, 0, unroll=2)
+
+    across = []
+    for a in (1, 0):
+        position = zh if a == 0 else 1 - zh
+        merge_y(position)
+        copy = remote(za.at[position], zi.at[position], Q_Z + a, at(dz=4))
+        copy.start()
+        across.append(copy)
+
+    def norm(position, logits, state_ref):
+        def group(g, carry):
+            stack = jnp.concatenate([za[position, g][None], zi[position, g][None], empty[0:2]], axis=0)
+            merged, _, _ = merge(stack, 4, True)
+            attf[g] = merged
+            return carry
+
+        lax.fori_loop(0, GROUPS, group, 0, unroll=2)
+        for g in range(GROUPS):
+            for j in range(PER_GROUP):
+                h = g * PER_GROUP + j
+                cols = slice(h * HEAD, (h + 1) * HEAD)
+                state = xrow[0:TOK, cols] + attf[g, j * TOK : (j + 1) * TOK, :]
+                state_ref[0:TOK, cols] = state.astype(BF16).astype(F32)
+        state = state_ref[0:TOK, :]
+        inv_rms = lax.rsqrt(jnp.mean(state * state, axis=1, keepdims=True) + 1e-05)
+        logit = jnp.broadcast_to(logits, (TOK, 128))
+        logit = jnp.sum(
+            jnp.where(iota((TOK, 128), 0) == iota((TOK, 128), 1), logit, 0.0), axis=1, keepdims=True
+        )
+        gate = 1.0 / (1.0 + jnp.exp(-logit))
+        xrow[0:TOK, :] = state * inv_rms * gain_ref[...].reshape(1, WIDTH).astype(F32) * gate
+        pack()
+        xg[y * 2 + position] = xf[...].astype(BF16)
+
+    ring = Ring(xg, X_AG)
+    xrow[0:TOK, :] = res_ref[0].astype(F32)
+    across[0].wait_recv()
+    norm(zh, lown[0:1, :], hid)
+    ring.go(1, 0)
+    res_copy.wait_recv()
+    logit_copy.wait_recv()
+    xf[...] = rfar[...].astype(F32)
+    unpack()
+    across[1].wait_recv()
+    norm(1 - zh, lfar[0:1, :], hid2)
+    ring.go(1, 1)
+    for d in (1, 2):
+        ring.pass_on(d, 0)
+        ring.pass_on(d, 1)
+    ring.pass_on(3, 0, (0,))
+    ring.pass_on(3, 1, (1,))
+    ring.got(3, 0, (1,))
+    ring.got(3, 1, (0,))
+    ring.got(4, 0, (0,))
+    ring.got(4, 1, (1,))
+    ring.end()
+    for copy in across:
+        copy.wait_send()
 
     rows_in = [xg[:, :, k * PART : (k + 1) * PART].reshape(256, PART) for k in range(3)]
     lanes = iota((96, 256), 1)
@@ -478,23 +543,24 @@
 
     own_block = pltpu.make_async_copy(sb.at[expert], rb.at[0, core, 0], local.at[24])
     own_block.start()
-    HALF = 3 * QUART // 2
+
+    def parity(cls):
+        return lax.rem(y + cls, 2)
 
     def routes(cls):
-        for dx in range(4):
-            if cls == 3:
-                yield slice(0, HALF), 2, dx, 12 + 2 * dx
-                yield slice(HALF, 2 * HALF), -2, dx, 13 + 2 * dx
-            elif (cls, dx) != (0, 0):
-                yield slice(0, 2 * HALF), CLASSES[cls], dx, cls * 4 + dx
+        if cls == 0:
+            for dx in (1, 2, 3):
+                yield 0, dx, dx - 1
+        else:
+            for i in (0, 1):
+                dz = CLASSES[cls] if cls < 3 else 2 - 4 * i
+                yield dz, 2 * i + parity(cls), 1 + 2 * cls + i
 
     sent = [[], [], [], []]
-    for cls in range(4):
-        for cols, dz, dx, sem in routes(cls):
+    for cls in (1, 2, 0, 3):
+        for dz, dx, index in routes(cls):
             to = lax.rem(zl + dz + 4, 4) * 4 + lax.rem(x + dx, 4)
-            copy = remote(
-                sb.at[to, :, cols], rb.at[cls, core, dx, :, cols], GO + sem, at(dz=dz, dx=dx)
-            )
+            copy = remote(sb.at[to], rb.at[cls, core, dx], GO + index, at(dz=dz, dx=dx))
             copy.start()
             sent[cls].append(copy)
 
@@ -527,49 +593,93 @@
         return results
 
     back = []
-    across_x = []
-    across_p = []
+    swaps = {}
+    across_x = {}
+    across_p = {}
+    partial = {}
+
+    def swap(cls):
+        swaps[cls] = []
+        for i, copy in enumerate(sent[cls]):
+            copy.wait_recv()
+            block = rb.at[cls, core, 2 * i + parity(cls)]
+            onward = remote(block, block, GO_Y + 2 * (cls - 1) + i, at(dy=1 - 2 * i))
+            onward.start()
+            swaps[cls].append(onward)
+
+    def share(cls):
+        if cls == 0:
+            for copy in sent[0]:
+                copy.wait_recv()
+            own_block.wait()
+        else:
+            for copy in swaps[cls]:
+                copy.wait_recv()
+        blocks = rb.at[cls, core]
+        across_x[cls] = remote(blocks, blocks, SIB_X + cls, at(flip=True))
+        across_x[cls].start()
+
+    def run(cls):
+        across_x[cls].wait_recv()
+        for j, part in enumerate(experts(rb[cls].reshape(128, 3 * QUART))):
+            pp[cls, :, :, :, j * QUART : (j + 1) * QUART] = part.reshape(2, 4, 16, QUART)
+        across_p[cls] = remote(pp.at[cls, 1 - core], qb.at[cls], SIB_P + cls, at(flip=True))
+        across_p[cls].start()
 
     def send_back(cls):
+        for dz, dx, index in routes(cls):
+            copy = remote(pp.at[cls, core, dx], rtn.at[expert], BACK + index, at(dz=-dz, dx=-dx))
+            copy.start()
+            back.append(copy)
+
+    def add_cores(cls):
         across_p[cls].wait_recv()
         pp[cls, core] = (pp[cls, core].astype(F32) + qb[cls].astype(F32)).astype(BF16)
-        for cols, dz, dx, sem in routes(cls):
+        if cls == 0:
+            send_back(0)
+            rtn[expert] = pp[0, core, 0]
+            return
+        partial[cls] = []
+        for i in (0, 1):
+            block = pp.at[cls, core, 2 * i + 1 - parity(cls)]
             copy = remote(
-                pp.at[cls, core, dx, :, cols],
-                rtn.at[expert, :, cols],
-                BACK + sem,
-                at(dz=-dz, dx=-dx),
+                block, yq.at[cls - 1, i], BACK_Y + 2 * (cls - 1) + i, at(dy=2 * i - 1)
             )
             copy.start()
-            back.append(copy)
+            partial[cls].append(copy)
+
+    def add_planes(cls):
+        for i in (0, 1):
+            partial[cls][i].wait_recv()
+            dx = 2 * i + parity(cls)
+            total = pp[cls, core, dx].astype(F32) + yq[cls - 1, i].astype(F32)
+            pp[cls, core, dx] = total.astype(BF16)
+        send_back(cls)
+
+    swap(1)
+    swap(2)
+    share(0)
+    run(0)
+    share(1)
+    swap(3)
+    run(1)
+    add_cores(0)
+    share(2)
+    run(2)
+    add_cores(1)
+    share(3)
+    run(3)
+    add_planes(1)
+    add_cores(2)
+    add_planes(2)
+    add_cores(3)
+    add_planes(3)
 
     for cls in range(4):
-        for copy in sent[cls]:
-            copy.wait_recv()
-        if cls == 0:
-            own_block.wait()
-        blocks = rb.at[cls, core]
-        copy = remote(blocks, blocks, SIB_X + cls, at(flip=True))
-        copy.start()
-        across_x.append(copy)
-        if cls > 0:
-            send_back(cls - 1)
-        copy.wait_recv()
-        for j, part in enumerate(experts(rb[cls].reshape(128, 3 * QUART))):
-            pp[cls, :, :, :, j * QUART : (j + 1) * QUART] = part.reshape(2, 4, 16, QUART)
-        copy = remote(pp.at[cls, 1 - core], qb.at[cls], SIB_P + cls, at(flip=True))
-        copy.start()
-        across_p.append(copy)
-    send_back(3)
-    own_back = pltpu.make_async_copy(pp.at[0, core, 0], rtn.at[expert], local.at[25])
-    own_back.start()
-
-    for cls in range(4):
-        for copy in sent[cls]:
+        for copy in sent[cls] + swaps.get(cls, []) + partial.get(cls, []):
             copy.wait_send()
         across_x[cls].wait_send()
         across_p[cls].wait_send()
-    own_back.wait()
     for copy in back:
         copy.wait()
 
@@ -620,13 +730,12 @@
         return total
 
     zo2[...] = add_up(1 - zh).astype(BF16)
-    across = remote(zo2, zi2, Y_RS + 10, at(dz=4))
+    across = remote(zo2, zi2, Y_Z, at(dz=4))
     across.start()
     xf[...] = add_up(zh)
     across.wait()
     xf[...] = xf[...] + zi2[...].astype(F32)
-    for (pr, pc), (wr, wc), n in pieces():
-        xrow[wr : wr + n, wc : wc + PART] = xf[pr : pr + n, pc : pc + PART]
+    unpack()
     out_ref[0] = (hid[0:TOK, :] + xrow[0:TOK, :]).astype(BF16)
 
 
@@ -658,13 +767,17 @@
             pltpu.VMEM((16,) + block, BF16),
             pltpu.VMEM((16,) + block, BF16),
             pltpu.VMEM((NY, 2) + block, BF16),
-            pltpu.VMEM(block, BF16),
-            pltpu.VMEM(block, BF16),
-            pltpu.VMEM(block, BF16),
+            pltpu.VMEM((2,) + block, BF16),
+            pltpu.VMEM((2,) + block, BF16),
             pltpu.VMEM((2, 2) + block, BF16),
             pltpu.VMEM((2,) + block, BF16),
             pltpu.VMEM((2, 2) + block, BF16),
             pltpu.VMEM(block, F32),
+            pltpu.VMEM((16, 3 * PART), BF16),
+            pltpu.VMEM((16, 3 * PART), BF16),
+            pltpu.VMEM((8, 128), F32),
+            pltpu.VMEM((8, 128), F32),
+            pltpu.VMEM((8, WIDTH), F32),
             pltpu.VMEM((8, WIDTH), F32),
             pltpu.VMEM((8, WIDTH), F32),
             pltpu.VMEM((16, 3 * PART), F32),
@@ -673,6 +786,7 @@
             pltpu.VMEM((4, 2, 4, 16, 3 * QUART), BF16),
             pltpu.VMEM((4, 2, 4, 16, 3 * QUART), BF16),
             pltpu.VMEM((4, 4, 16, 3 * QUART), BF16),
+            pltpu.VMEM((3, 2, 16, 3 * QUART), BF16),
             pltpu.VMEM(slots, BF16),
             pltpu.VMEM((16, 16, 3 * PART), BF16),
             pltpu.VMEM((5, 2, 16, 3 * PART), BF16),
@@ -686,7 +800,7 @@
             pltpu.VMEM((GROUPS, KEYS, HEAD), BF16),
             pltpu.VMEM((GROUPS, KEYS, 2 * HEAD), BF16),
             pltpu.VMEM((2, 16, GROUPS * HEAD), F32),
-            pltpu.VMEM((128, KEYS), F32),
+            pltpu.VMEM((192, KEYS), F32),
             pltpu.SemaphoreType.DMA((N_SEM,)),
             pltpu.SemaphoreType.DMA((N_SEM,)),
             pltpu.SemaphoreType.DMA((26,)),

time: 169 us -> 156 us (0.923)
  the two profiles are of different devices: /device:TPU:200 before, /device:TPU:8 now
where the time goes in v3:
time: 156 us
  Pallas kernels  154 us (99%)
    pallas_call x1, Pallas kernels, body(): pl.pallas_call(kernel, out_shape=jax.ShapeDtypeStruct((1, TOK, WIDTH), BF...  154 us

profile of v3, /device:TPU:8, one launch (start us, length us, event | category | flops | bytes accessed | tf_op | source)
XLA Modules:
  0.0 155.9 jit_solution(2265924483530719806)
XLA Ops:
  0.7 153.7 %shard_map.109 = bf16[1,6,5120]{2,1,0:T(8,128)(2,1)} custom-call(bf16[1,6,5120]{2,1,0:T(8,128)(2,1)} %q_ref.1, bf16[1,6,2,1024]{3,2,1,0:T(2,128)(2,1)} %bitcast.2, bf16[2,1,256,1024]{3,2,1,0:T(8,128)(2,1)} %cache_ref.1, s32[1]{0:T(128)S(6)} %copy.13.len_ref, bf16[1,6,5120]{2,1,0:T(8,128)(2,1)} %res_ref.1, bf16[5120]{0:T(1024)(128)(2,1)} %gain_ref.1, ...), custom_call_target="tpu_custom_call" | custom-call | tf_op jit(solution)/shard_map/pallas_call | solution.py:760
  154.4 1.5 copy.14

commit v4 on v3

--- a/solution.py
+++ b/solution.py
@@ -29,13 +29,11 @@
 X_AG = 32
 GO = 48
 GO_Y = 57
-SIB_X = 63
-SIB_P = 67
+WEIGHTS = 63
 BACK_Y = 71
 BACK = 77
 Y_RS = 86
-Y_Z = 96
-N_SEM = 97
+N_SEM = 119
 CLASSES = (0, 1, -1, 2)
 
 
@@ -99,7 +97,6 @@
     sb,
     rb,
     pp,
-    qb,
     yq,
     rtn,
     rsb,
@@ -143,21 +140,19 @@
             device_id_type=MESH,
         )
 
-    copies = [
-        pltpu.make_async_copy(wg_ref.at[0], wgu.at[:, 0:128], local.at[0]),
-        pltpu.make_async_copy(wu_ref.at[0], wgu.at[:, 128:256], local.at[1]),
+    def of_core(start):
+        return pl.ds(pl.multiple_of(start + core * 128, 128), 128)
+
+    parts = [
+        (wg_ref.at[0], wgu.at[:, of_core(0)]),
+        (wu_ref.at[0], wgu.at[:, of_core(256)]),
     ]
     for j in range(3):
-        copies.append(
-            pltpu.make_async_copy(
-                wd_ref.at[0, :, j * QUART : (j + 1) * QUART], wdx.at[j, 0:128], local.at[2 + 2 * j]
-            )
-        )
-        copies.append(
-            pltpu.make_async_copy(
-                wd_ref.at[0, :, 3 * QUART : 4 * QUART], wdx.at[j, 128:256], local.at[3 + 2 * j]
-            )
-        )
+        parts.append((wd_ref.at[0, :, j * QUART : (j + 1) * QUART], wdx.at[j, of_core(0)]))
+        parts.append((wd_ref.at[0, :, 3 * QUART : 4 * QUART], wdx.at[j, of_core(256)]))
+    copies = [
+        pltpu.make_async_copy(src, dst, local.at[i]) for i, (src, dst) in enumerate(parts)
+    ]
     cache_copies = []
     for g in range(GROUPS):
         cols = slice(g * HEAD, (g + 1) * HEAD)
@@ -341,8 +336,9 @@
         return copy
 
     def ship_near(src, dst, base):
-        ship(src.at[pair_of(1)], dst.at[1], base, 1)
-        ship(src.at[pair_of(-1)], dst.at[2], base + 1, -1)
+        up = ship(src.at[pair_of(1)], dst.at[1], base, 1)
+        down = ship(src.at[pair_of(-1)], dst.at[2], base + 1, -1)
+        return [up, down]
 
     def ship_three(src, dst, base):
         up = ship(src.at[pair_of(3)], dst.at[0], base + 2, 1)
@@ -366,13 +362,19 @@
         return carry
 
     lax.fori_loop(0, GROUPS, settle_rin, 0)
-    def both(d):
-        return [block_of(d, 0), block_of(d, 1)]
-
     ring.pass_on(1, 0)
+    attend([block_of(0, 0), block_of(-1, 0), block_of(1, 0)])
+    ring.pass_on(2, 0)
     near.wait_recv()
     ring.go(1, 1)
-    ring.pass_on(2, 0)
+    weight_copies = []
+    for i, (src, dst) in enumerate(parts):
+        weight_copies.append(remote(src, dst, WEIGHTS + i, at(flip=True)))
+        weight_copies[i].start()
+    attend([block_of(-2, 0), block_of(2, 0), block_of(0, 1)])
+    rin[0] = pw[pair_of(0)]
+    ring.pass_on(3, 0, (0,))
+    ring.got(3, 0, (1,))
     ring.pass_on(1, 1)
     opposite.wait_recv()
     beyond = []
@@ -381,19 +383,16 @@
         copy = remote(block, block, Q_AG + 2 + (way * 4 + 2) * 2 + 1, at(dy=sign))
         copy.start()
         beyond.append(copy)
-    attend(both(0) + both(-1) + both(1))
-    rin[0] = pw[pair_of(0)]
+    attend([block_of(-3, 0), block_of(3, 0), block_of(-1, 1), block_of(1, 1)])
     ship_near(pw, rin, Q_RS)
-    ring.pass_on(3, 0, (0,))
-    ring.got(3, 0, (1,))
-    ring.got(2, 1)
-    attend(both(-2) + both(2))
+    ring.got(4, 0, (0,))
     for copy in beyond:
         copy.wait_recv()
-    ring.got(4, 0, (0,))
-    attend(both(-3) + both(3) + both(4))
+    attend([block_of(4, 0), block_of(4, 1), block_of(-3, 1), block_of(3, 1)])
     far[3] = ship_three(pw, r3, Q_RS)
     far[4] = ship_four(pw, r4, Q_RS)
+    ring.got(2, 1)
+    attend([block_of(-2, 1), block_of(2, 1)])
     ring.end()
     for copy in beyond + [near, opposite, res_copy, logit_copy]:
         copy.wait_send()
@@ -541,7 +540,7 @@
             start = j * QUART + half * PART
             sb[:, :, start : start + PART] = total.astype(BF16).reshape(16, 16, PART)
 
-    own_block = pltpu.make_async_copy(sb.at[expert], rb.at[0, core, 0], local.at[24])
+    own_block = pltpu.make_async_copy(sb.at[expert], rb.at[0, 0], local.at[24])
     own_block.start()
 
     def parity(cls):
@@ -560,17 +559,17 @@
     for cls in (1, 2, 0, 3):
         for dz, dx, index in routes(cls):
             to = lax.rem(zl + dz + 4, 4) * 4 + lax.rem(x + dx, 4)
-            copy = remote(sb.at[to], rb.at[cls, core, dx], GO + index, at(dz=dz, dx=dx))
+            copy = remote(sb.at[to], rb.at[cls, dx], GO + index, at(dz=dz, dx=dx))
             copy.start()
             sent[cls].append(copy)
 
-    for copy in copies:
+    for copy in copies + weight_copies:
         copy.wait()
 
     def experts(rows):
         n = rows.shape[0]
         main = jnp.dot(rows, wgu[0 : 3 * QUART, :], preferred_element_type=F32)
-        r = iota((n, 256), 0) & 15
+        r = iota((n, 512), 0) & 15
         tail = None
         for j in (2, 1, 0):
             part = jnp.dot(
@@ -581,9 +580,9 @@
             part = pltpu.roll(part, n - 12 + 4 * j, 0)
             tail = part if tail is None else jnp.where(r < 4 * (j + 1), part, tail)
         both = main + tail
-        gate_out, up_out = both[:, 0:128], both[:, 128:256]
+        gate_out, up_out = both[:, 0:256], both[:, 256:512]
         act = gate_out / (1.0 + jnp.exp(-gate_out)) * up_out
-        r = iota((n, 128), 0) & 15
+        r = iota((n, 256), 0) & 15
         act = jnp.where(r < 12, act, 0.0).astype(BF16).astype(F32)
         results = []
         for j in range(3):
@@ -594,54 +593,34 @@
 
     back = []
     swaps = {}
-    across_x = {}
-    across_p = {}
     partial = {}
 
     def swap(cls):
         swaps[cls] = []
         for i, copy in enumerate(sent[cls]):
             copy.wait_recv()
-            block = rb.at[cls, core, 2 * i + parity(cls)]
+            block = rb.at[cls, 2 * i + parity(cls)]
             onward = remote(block, block, GO_Y + 2 * (cls - 1) + i, at(dy=1 - 2 * i))
             onward.start()
             swaps[cls].append(onward)
 
-    def share(cls):
-        if cls == 0:
-            for copy in sent[0]:
-                copy.wait_recv()
-            own_block.wait()
-        else:
-            for copy in swaps[cls]:
-                copy.wait_recv()
-        blocks = rb.at[cls, core]
-        across_x[cls] = remote(blocks, blocks, SIB_X + cls, at(flip=True))
-        across_x[cls].start()
-
-    def run(cls):
-        across_x[cls].wait_recv()
-        for j, part in enumerate(experts(rb[cls].reshape(128, 3 * QUART))):
-            pp[cls, :, :, :, j * QUART : (j + 1) * QUART] = part.reshape(2, 4, 16, QUART)
-        across_p[cls] = remote(pp.at[cls, 1 - core], qb.at[cls], SIB_P + cls, at(flip=True))
-        across_p[cls].start()
+    def run(first, count):
+        rows = rb[first : first + count].reshape(64 * count, 3 * QUART)
+        for j, part in enumerate(experts(rows)):
+            pp[first : first + count, :, :, j * QUART : (j + 1) * QUART] = part.reshape(
+                count, 4, 16, QUART
+            )
 
     def send_back(cls):
         for dz, dx, index in routes(cls):
-            copy = remote(pp.at[cls, core, dx], rtn.at[expert], BACK + index, at(dz=-dz, dx=-dx))
+            copy = remote(pp.at[cls, dx], rtn.at[expert], BACK + index, at(dz=-dz, dx=-dx))
             copy.start()
             back.append(copy)
 
-    def add_cores(cls):
-        across_p[cls].wait_recv()
-        pp[cls, core] = (pp[cls, core].astype(F32) + qb[cls].astype(F32)).astype(BF16)
-        if cls == 0:
-            send_back(0)
-            rtn[expert] = pp[0, core, 0]
-            return
+    def give(cls):
         partial[cls] = []
         for i in (0, 1):
-            block = pp.at[cls, core, 2 * i + 1 - parity(cls)]
+            block = pp.at[cls, 2 * i + 1 - parity(cls)]
             copy = remote(
                 block, yq.at[cls - 1, i], BACK_Y + 2 * (cls - 1) + i, at(dy=2 * i - 1)
             )
@@ -652,37 +631,40 @@
         for i in (0, 1):
             partial[cls][i].wait_recv()
             dx = 2 * i + parity(cls)
-            total = pp[cls, core, dx].astype(F32) + yq[cls - 1, i].astype(F32)
-            pp[cls, core, dx] = total.astype(BF16)
+            total = pp[cls, dx].astype(F32) + yq[cls - 1, i].astype(F32)
+            pp[cls, dx] = total.astype(BF16)
         send_back(cls)
 
     swap(1)
     swap(2)
-    share(0)
-    run(0)
-    share(1)
+    for copy in sent[0]:
+        copy.wait_recv()
+    own_block.wait()
+    run(0, 1)
+    send_back(0)
+    rtn[expert] = pp[0, 0]
     swap(3)
-    run(1)
-    add_cores(0)
-    share(2)
-    run(2)
-    add_cores(1)
-    share(3)
-    run(3)
+    for cls in (1, 2):
+        for copy in swaps[cls]:
+            copy.wait_recv()
+    run(1, 2)
+    give(1)
+    give(2)
+    for copy in swaps[3]:
+        copy.wait_recv()
+    run(3, 1)
+    give(3)
     add_planes(1)
-    add_cores(2)
     add_planes(2)
-    add_cores(3)
     add_planes(3)
 
     for cls in range(4):
         for copy in sent[cls] + swaps.get(cls, []) + partial.get(cls, []):
             copy.wait_send()
-        across_x[cls].wait_send()
-        across_p[cls].wait_send()
     for copy in back:
         copy.wait()
 
+    due = []
     lanes = iota((256, 128), 1)
     for k in range(3):
         tok, _ = item_of(iota((256, 128), 0), k)
@@ -699,44 +681,54 @@
                 start = j * QUART + half * PART
                 source = rtn[:, :, start : start + PART].reshape(256, PART)
                 total = total + jnp.dot(pick, source, preferred_element_type=F32)
-        rsb[:, :, k * PART : (k + 1) * PART] = total.astype(BF16).reshape(16, 16, PART)
-
-    far[3] = ship_three(rsb, f3, Y_RS)
-    far[4] = ship_four(rsb, f4, Y_RS)
-    ship_near(rsb, rsi, Y_RS)
-    rsi[0] = rsb[pair_of(0)]
-    for side in (0, 1):
-        far[3][side].wait_recv()
-        for a in (1 - side, side):
-            position = zh if a == 0 else 1 - zh
-            total = rsb[block_of(2 - 4 * side, a)].astype(F32) + f3[side, position].astype(F32)
-            if a == side:
-                far[4][side].wait_recv()
-                total = total + f4[side].astype(F32)
-            fm[side, a] = total.astype(BF16)
-            ship(
-                fm.at[side, a], rsi.at[3 + side, position], Y_RS + 6 + 2 * side + a, 2 - 4 * side
-            )
-    for copy in scatters:
-        copy.wait_send()
-    for copy in scatters:
-        if not any(copy is other for other in far[3] + far[4]):
+        rsb[k] = total.astype(BF16).reshape(16, 16, PART)
+        base = Y_RS + 11 * k
+        far[3, k] = ship_three(rsb.at[k], f3.at[k], base)
+        far[4, k] = ship_four(rsb.at[k], f4.at[k], base)
+        due.append([])
+        due[k] += ship_near(rsb.at[k], rsi.at[k], base)
+        rsi[k, 0] = rsb[k, pair_of(0)]
+
+    for k in range(3):
+        for side in (0, 1):
+            far[3, k][side].wait_recv()
+            for a in (1 - side, side):
+                position = zh if a == 0 else 1 - zh
+                total = rsb[k, block_of(2 - 4 * side, a)].astype(F32)
+                total = total + f3[k, side, position].astype(F32)
+                if a == side:
+                    far[4, k][side].wait_recv()
+                    total = total + f4[k, side].astype(F32)
+                fm[k, side, a] = total.astype(BF16)
+                copy = ship(
+                    fm.at[k, side, a],
+                    rsi.at[k, 3 + side, position],
+                    Y_RS + 11 * k + 6 + 2 * side + a,
+                    2 - 4 * side,
+                )
+                due[k].append(copy)
+
+    def add_up(k, block):
+        total = rsi[k, 0, block].astype(F32)
+        for i in range(1, 5):
+            total = total + rsi[k, i, block].astype(F32)
+        return total
+
+    across = []
+    for k in range(3):
+        for copy in due[k]:
             copy.wait_recv()
-
-    def add_up(block):
-        total = rsi[0, block].astype(F32)
-        for i in range(1, 5):
-            total = total + rsi[i, block].astype(F32)
-        return total
-
-    zo2[...] = add_up(1 - zh).astype(BF16)
-    across = remote(zo2, zi2, Y_Z, at(dz=4))
-    across.start()
-    xf[...] = add_up(zh)
-    across.wait()
-    xf[...] = xf[...] + zi2[...].astype(F32)
+        zo2[k] = add_up(k, 1 - zh).astype(BF16)
+        across.append(remote(zo2.at[k], zi2.at[k], Y_RS + 11 * k + 10, at(dz=4)))
+        across[k].start()
+    for k in range(3):
+        total = add_up(k, zh)
+        across[k].wait_recv()
+        xf[:, k * PART : (k + 1) * PART] = total + zi2[k].astype(F32)
     unpack()
     out_ref[0] = (hid[0:TOK, :] + xrow[0:TOK, :]).astype(BF16)
+    for copy in scatters + across:
+        copy.wait_send()
 
 
 def body(
@@ -783,24 +775,23 @@
             pltpu.VMEM((16, 3 * PART), F32),
             pltpu.VMEM((16, 16, 3 * PART), BF16),
             pltpu.VMEM(slots, BF16),
-            pltpu.VMEM((4, 2, 4, 16, 3 * QUART), BF16),
-            pltpu.VMEM((4, 2, 4, 16, 3 * QUART), BF16),
+            pltpu.VMEM((4, 4, 16, 3 * QUART), BF16),
             pltpu.VMEM((4, 4, 16, 3 * QUART), BF16),
             pltpu.VMEM((3, 2, 16, 3 * QUART), BF16),
             pltpu.VMEM(slots, BF16),
-            pltpu.VMEM((16, 16, 3 * PART), BF16),
-            pltpu.VMEM((5, 2, 16, 3 * PART), BF16),
-            pltpu.VMEM((2, 2, 16, 3 * PART), BF16),
-            pltpu.VMEM((2, 16, 3 * PART), BF16),
-            pltpu.VMEM((2, 2, 16, 3 * PART), BF16),
-            pltpu.VMEM((16, 3 * PART), BF16),
-            pltpu.VMEM((16, 3 * PART), BF16),
-            pltpu.VMEM((WIDTH, 256), BF16),
-            pltpu.VMEM((3, 256, QUART), BF16),
+            pltpu.VMEM((3, 16, 16, PART), BF16),
+            pltpu.VMEM((3, 5, 2, 16, PART), BF16),
+            pltpu.VMEM((3, 2, 2, 16, PART), BF16),
+            pltpu.VMEM((3, 2, 16, PART), BF16),
+            pltpu.VMEM((3, 2, 2, 16, PART), BF16),
+            pltpu.VMEM((3, 16, PART), BF16),
+            pltpu.VMEM((3, 16, PART), BF16),
+            pltpu.VMEM((WIDTH, 512), BF16),
+            pltpu.VMEM((3, 512, QUART), BF16),
             pltpu.VMEM((GROUPS, KEYS, HEAD), BF16),
             pltpu.VMEM((GROUPS, KEYS, 2 * HEAD), BF16),
             pltpu.VMEM((2, 16, GROUPS * HEAD), F32),
-            pltpu.VMEM((192, KEYS), F32),
+            pltpu.VMEM((128, KEYS), F32),
             pltpu.SemaphoreType.DMA((N_SEM,)),
             pltpu.SemaphoreType.DMA((N_SEM,)),
             pltpu.SemaphoreType.DMA((26,)),

time: 156 us -> 142 us (0.910)
  the two profiles are of different devices: /device:TPU:8 before, /device:TPU:24 now
where the time goes in v4:
time: 142 us
  Pallas kernels  140 us (99%)
  local copies, waits for them, and re-layouts  1.53 us (1%)
    pallas_call x1, Pallas kernels, body(): pl.pallas_call(kernel, out_shape=jax.ShapeDtypeStruct((1, TOK, WIDTH), BF...  140 us

profile of v4, /device:TPU:24, one launch (start us, length us, event | category | flops | bytes accessed | tf_op | source)
XLA Modules:
  0.0 142.0 jit_solution(12543394562632938356)
XLA Ops:
  0.7 139.8 %shard_map.109 = bf16[1,6,5120]{2,1,0:T(8,128)(2,1)} custom-call(bf16[1,6,5120]{2,1,0:T(8,128)(2,1)} %q_ref.1, bf16[1,6,2,1024]{3,2,1,0:T(2,128)(2,1)} %bitcast.2, bf16[2,1,256,1024]{3,2,1,0:T(8,128)(2,1)} %cache_ref.1, s32[1]{0:T(128)S(6)} %copy.13.len_ref, bf16[1,6,5120]{2,1,0:T(8,128)(2,1)} %res_ref.1, bf16[5120]{0:T(1024)(128)(2,1)} %gain_ref.1, ...), custom_call_target="tpu_custom_call" | custom-call | tf_op jit(solution)/shard_map/pallas_call | solution.py:752
  140.4 1.5 %copy.14 = bf16[1,6,5120]{2,1,0:T(8,128)(2,1)} copy(bf16[1,6,5120]{2,1,0:T(8,128)(2,1)} %shard_map.109) | data formatting | bytes 122880

commit v5 on v4

--- a/solution.py
+++ b/solution.py
@@ -115,6 +115,7 @@
     send,
     recv,
     local,
+    know,
 ):
     ctx = lax.axis_index("ctx")
     ep = lax.axis_index("ep")
@@ -170,11 +171,16 @@
         copy.start()
 
     barrier = pltpu.get_barrier_semaphore()
-    partners = [at(dy=d) for d in (1, -1, 2, -2)] + [at(dz=4), at(dy=4, dz=4), at(flip=True)]
-    for dz in (0, 1, -1, 2, -2):
-        partners += [at(dz=dz, dx=dx) for dx in range(4) if (dz, dx) != (0, 0)]
+    beside_x = [at(dx=1), at(dx=-1)]
+    beside_z = [at(dz=1), at(dz=-1)]
+    beside_y = [at(dy=1), at(dy=-1)]
+    partners = [at(dz=4), at(dy=4)] + beside_y + beside_x + beside_z + [at(flip=True)]
     for device in partners:
         pl.semaphore_signal(barrier, inc=1, device_id=device, device_id_type=MESH)
+
+    def tell(step, devices):
+        for device in devices:
+            pl.semaphore_signal(know.at[step], inc=1, device_id=device, device_id_type=MESH)
 
     qf[...] = jnp.zeros_like(qf)
     queries = q_ref[0].astype(F32)
@@ -223,8 +229,9 @@
     ring.go(1, 0)
     near = remote(own, own, Q_AG, at(dz=4))
     near.start()
-    opposite = remote(own, own, Q_AG + 1, at(dy=4, dz=4))
-    opposite.start()
+    partner_block = qg.at[block_of(0, 1)]
+    opposite = remote(partner_block, partner_block, Q_AG + 1, at(dy=4))
+    tell(0, beside_y + beside_x + beside_z)
 
     def pieces():
         for e in range(6):
@@ -322,7 +329,7 @@
                 pw[block, g] = packed[i]
             return carry
 
-        lax.fori_loop(0, GROUPS, group, 0, unroll=2)
+        lax.fori_loop(0, GROUPS, group, 0, unroll=4)
 
     scatters = []
 
@@ -364,14 +371,19 @@
     lax.fori_loop(0, GROUPS, settle_rin, 0)
     ring.pass_on(1, 0)
     attend([block_of(0, 0), block_of(-1, 0), block_of(1, 0)])
+    pl.semaphore_wait(know.at[0], 6)
+    tell(1, beside_x + beside_z)
     ring.pass_on(2, 0)
     near.wait_recv()
+    opposite.start()
     ring.go(1, 1)
     weight_copies = []
     for i, (src, dst) in enumerate(parts):
         weight_copies.append(remote(src, dst, WEIGHTS + i, at(flip=True)))
         weight_copies[i].start()
     attend([block_of(-2, 0), block_of(2, 0), block_of(0, 1)])
+    pl.semaphore_wait(know.at[1], 4)
+    tell(2, beside_x)
     rin[0] = pw[pair_of(0)]
     ring.pass_on(3, 0, (0,))
     ring.got(3, 0, (1,))
@@ -384,6 +396,7 @@
         copy.start()
         beyond.append(copy)
     attend([block_of(-3, 0), block_of(3, 0), block_of(-1, 1), block_of(1, 1)])
+    pl.semaphore_wait(know.at[2], 2)
     ship_near(pw, rin, Q_RS)
     ring.got(4, 0, (0,))
     for copy in beyond:
@@ -442,7 +455,7 @@
                 mg[side, a, g] = merged_block(stack, 4)
                 return carry
 
-            lax.fori_loop(0, GROUPS, group, 0)
+            lax.fori_loop(0, GROUPS, group, 0, unroll=8)
             position = zh if a == 0 else 1 - zh
             ship(
                 mg.at[side, a], rin.at[3 + side, position], Q_RS + 6 + 2 * side + a, 2 - 4 * side
@@ -459,7 +472,7 @@
             za[block, g] = merged_block(rin[:, block, g], NY)
             return carry
 
-        lax.fori_loop(0, GROUPS, group, 0, unroll=2)
+        lax.fori_loop(0, GROUPS, group, 0, unroll=8)
 
     across = []
     for a in (1, 0):
@@ -476,7 +489,7 @@
             attf[g] = merged
             return carry
 
-        lax.fori_loop(0, GROUPS, group, 0, unroll=2)
+        lax.fori_loop(0, GROUPS, group, 0, unroll=8)
         for g in range(GROUPS):
             for j in range(PER_GROUP):
                 h = g * PER_GROUP + j
@@ -795,6 +808,7 @@
             pltpu.SemaphoreType.DMA((N_SEM,)),
             pltpu.SemaphoreType.DMA((N_SEM,)),
             pltpu.SemaphoreType.DMA((26,)),
+            pltpu.SemaphoreType.REGULAR((3,)),
         ],
         compiler_params=pltpu.CompilerParams(
             collective_id=0, has_side_effects=True, vmem_limit_bytes=56 * 1024 * 1024

time: 142 us -> 135 us (0.951)
  the two profiles are of different devices: /device:TPU:24 before, /device:TPU:2 now
where the time goes in v5:
time: 135 us
  Pallas kernels  133 us (99%)
  local copies, waits for them, and re-layouts  1.53 us (1%)
    pallas_call x1, Pallas kernels, body(): pl.pallas_call(kernel, out_shape=jax.ShapeDtypeStruct((1, TOK, WIDTH), BF...  133 us

profile of v5, /device:TPU:2, one launch (start us, length us, event | category | flops | bytes accessed | tf_op | source)
XLA Modules:
  0.0 134.8 jit_solution(5053616197798950325)
XLA Ops:
  0.7 132.6 %shard_map.109 = bf16[1,6,5120]{2,1,0:T(8,128)(2,1)} custom-call(bf16[1,6,5120]{2,1,0:T(8,128)(2,1)} %q_ref.1, bf16[1,6,2,1024]{3,2,1,0:T(2,128)(2,1)} %bitcast.2, bf16[2,1,256,1024]{3,2,1,0:T(8,128)(2,1)} %cache_ref.1, s32[1]{0:T(128)S(6)} %copy.13.len_ref, bf16[1,6,5120]{2,1,0:T(8,128)(2,1)} %res_ref.1, bf16[5120]{0:T(1024)(128)(2,1)} %gain_ref.1, ...), custom_call_target="tpu_custom_call" | custom-call | tf_op jit(solution)/shard_map/pallas_call | solution.py:765
  133.3 1.5 %copy.14 = bf16[1,6,5120]{2,1,0:T(8,128)(2,1)} copy(bf16[1,6,5120]{2,1,0:T(8,128)(2,1)} %shard_map.109) | data formatting | bytes 122880

commit v6 on v5

--- a/solution.py
+++ b/solution.py
@@ -28,13 +28,14 @@
 Q_Z = 30
 X_AG = 32
 GO = 48
-GO_Y = 57
-WEIGHTS = 63
-BACK_Y = 71
-BACK = 77
-Y_RS = 86
-N_SEM = 119
+GO_Y = 56
+WEIGHTS = 64
+BACK_Y = 72
+BACK = 80
+Y_RS = 88
+N_SEM = 121
 CLASSES = (0, 1, -1, 2)
+ORDER = (1, 2, 3, 0)
 
 
 def iota(shape, dim):
@@ -560,20 +561,24 @@
         return lax.rem(y + cls, 2)
 
     def routes(cls):
-        if cls == 0:
-            for dx in (1, 2, 3):
-                yield 0, dx, dx - 1
+        for i in (0, 1):
+            dz = CLASSES[cls] if cls < 3 else 2 - 4 * i
+            yield dz, 2 * i + parity(cls), 2 * cls + i
+
+    odd, even = parity(0) == 1, parity(0) == 0
+
+    def where_sent(cls, i, act, plane=odd):
+        if (cls, i) == (0, 0):
+            pl.when(plane)(act)
         else:
-            for i in (0, 1):
-                dz = CLASSES[cls] if cls < 3 else 2 - 4 * i
-                yield dz, 2 * i + parity(cls), 1 + 2 * cls + i
+            act()
 
     sent = [[], [], [], []]
-    for cls in (1, 2, 0, 3):
-        for dz, dx, index in routes(cls):
+    for cls in ORDER:
+        for i, (dz, dx, index) in enumerate(routes(cls)):
             to = lax.rem(zl + dz + 4, 4) * 4 + lax.rem(x + dx, 4)
             copy = remote(sb.at[to], rb.at[cls, dx], GO + index, at(dz=dz, dx=dx))
-            copy.start()
+            where_sent(cls, i, copy.start)
             sent[cls].append(copy)
 
     for copy in copies + weight_copies:
@@ -604,18 +609,26 @@
             results.append(jnp.dot(left, wdx[j], preferred_element_type=F32).astype(BF16))
         return results
 
-    back = []
+    back = {}
     swaps = {}
     partial = {}
 
     def swap(cls):
         swaps[cls] = []
         for i, copy in enumerate(sent[cls]):
-            copy.wait_recv()
             block = rb.at[cls, 2 * i + parity(cls)]
-            onward = remote(block, block, GO_Y + 2 * (cls - 1) + i, at(dy=1 - 2 * i))
-            onward.start()
+            onward = remote(block, block, GO_Y + 2 * cls + i, at(dy=1 - 2 * i))
+
+            def pass_on(copy=copy, onward=onward):
+                copy.wait_recv()
+                onward.start()
+
+            where_sent(cls, i, pass_on)
             swaps[cls].append(onward)
+
+    def swapped(cls):
+        for i, onward in enumerate(swaps[cls]):
+            where_sent(cls, i, onward.wait_recv, even)
 
     def run(first, count):
         rows = rb[first : first + count].reshape(64 * count, 3 * QUART)
@@ -624,58 +637,52 @@
                 count, 4, 16, QUART
             )
 
-    def send_back(cls):
-        for dz, dx, index in routes(cls):
-            copy = remote(pp.at[cls, dx], rtn.at[expert], BACK + index, at(dz=-dz, dx=-dx))
-            copy.start()
-            back.append(copy)
-
     def give(cls):
         partial[cls] = []
         for i in (0, 1):
             block = pp.at[cls, 2 * i + 1 - parity(cls)]
-            copy = remote(
-                block, yq.at[cls - 1, i], BACK_Y + 2 * (cls - 1) + i, at(dy=2 * i - 1)
-            )
-            copy.start()
+            copy = remote(block, yq.at[cls, i], BACK_Y + 2 * cls + i, at(dy=2 * i - 1))
+            where_sent(cls, i, copy.start, even)
             partial[cls].append(copy)
 
-    def add_planes(cls):
-        for i in (0, 1):
-            partial[cls][i].wait_recv()
-            dx = 2 * i + parity(cls)
-            total = pp[cls, dx].astype(F32) + yq[cls - 1, i].astype(F32)
-            pp[cls, dx] = total.astype(BF16)
-        send_back(cls)
-
-    swap(1)
-    swap(2)
-    for copy in sent[0]:
-        copy.wait_recv()
+    def send_back(cls):
+        back[cls] = []
+        for i, (dz, dx, index) in enumerate(routes(cls)):
+            copy = remote(pp.at[cls, dx], rtn.at[expert], BACK + index, at(dz=-dz, dx=-dx))
+
+            def add_planes(i=i, dx=dx, copy=copy):
+                partial[cls][i].wait_recv()
+                total = pp[cls, dx].astype(F32) + yq[cls, i].astype(F32)
+                pp[cls, dx] = total.astype(BF16)
+                copy.start()
+
+            where_sent(cls, i, add_planes)
+            back[cls].append(copy)
+
     own_block.wait()
-    run(0, 1)
-    send_back(0)
-    rtn[expert] = pp[0, 0]
-    swap(3)
-    for cls in (1, 2):
-        for copy in swaps[cls]:
-            copy.wait_recv()
+    for cls in ORDER:
+        swap(cls)
+    swapped(1)
+    swapped(2)
     run(1, 2)
     give(1)
     give(2)
-    for copy in swaps[3]:
-        copy.wait_recv()
+    swapped(3)
     run(3, 1)
     give(3)
-    add_planes(1)
-    add_planes(2)
-    add_planes(3)
+    swapped(0)
+    run(0, 1)
+    give(0)
+    rtn[expert] = pp[0, 0]
+    for cls in ORDER:
+        send_back(cls)
 
     for cls in range(4):
-        for copy in sent[cls] + swaps.get(cls, []) + partial.get(cls, []):
-            copy.wait_send()
-    for copy in back:
-        copy.wait()
+        for i in (0, 1):
+            where_sent(cls, i, sent[cls][i].wait_send)
+            where_sent(cls, i, swaps[cls][i].wait_send)
+            where_sent(cls, i, partial[cls][i].wait_send, even)
+            where_sent(cls, i, back[cls][i].wait)
 
     due = []
     lanes = iota((256, 128), 1)
@@ -790,7 +797,7 @@
             pltpu.VMEM(slots, BF16),
             pltpu.VMEM((4, 4, 16, 3 * QUART), BF16),
             pltpu.VMEM((4, 4, 16, 3 * QUART), BF16),
-            pltpu.VMEM((3, 2, 16, 3 * QUART), BF16),
+            pltpu.VMEM((4, 2, 16, 3 * QUART), BF16),
             pltpu.VMEM(slots, BF16),
             pltpu.VMEM((3, 16, 16, PART), BF16),
             pltpu.VMEM((3, 5, 2, 16, PART), BF16),

time: 135 us -> 129 us (0.956)
  the two profiles are of different devices: /device:TPU:2 before, /device:TPU:8 now
where the time goes in v6:
time: 129 us
  Pallas kernels  127 us (98%)
  local copies, waits for them, and re-layouts  1.53 us (1%)
    pallas_call x1, Pallas kernels, body(): pl.pallas_call(kernel, out_shape=jax.ShapeDtypeStruct((1, TOK, WIDTH), BF...  127 us

profile of v6, /device:TPU:8, one launch (start us, length us, event | category | flops | bytes accessed | tf_op | source)
XLA Modules:
  0.0 129.0 jit_solution(8610235368090952970)
XLA Ops:
  0.7 126.8 %shard_map.109 = bf16[1,6,5120]{2,1,0:T(8,128)(2,1)} custom-call(bf16[1,6,5120]{2,1,0:T(8,128)(2,1)} %q_ref.1, bf16[1,6,2,1024]{3,2,1,0:T(2,128)(2,1)} %bitcast.2, bf16[2,1,256,1024]{3,2,1,0:T(8,128)(2,1)} %cache_ref.1, s32[1]{0:T(128)S(6)} %copy.13.len_ref, bf16[1,6,5120]{2,1,0:T(8,128)(2,1)} %res_ref.1, bf16[5120]{0:T(1024)(128)(2,1)} %gain_ref.1, ...), custom_call_target="tpu_custom_call" | custom-call | tf_op jit(solution)/shard_map/pallas_call | solution.py:772
  127.5 1.5 %copy.14 = bf16[1,6,5120]{2,1,0:T(8,128)(2,1)} copy(bf16[1,6,5120]{2,1,0:T(8,128)(2,1)} %shard_map.109) | data formatting | bytes 122880

commit v7 on v6

--- a/solution.py
+++ b/solution.py
@@ -541,21 +541,20 @@
         lane_slots.append(
             jnp.sum(jnp.where(iota((96, 256), 0) == tok, slot_col, 0.0), axis=0, keepdims=True)
         )
-    for j in range(3):
-        for half in range(2):
-            target, eighth_row = slot_of(iota((256, 256), 0), j, half)
-            target = target.astype(F32)
-            total = jnp.zeros((256, PART), F32)
-            for k in thirds_for(j, half):
-                _, eighth_lane = item_of(iota((256, 256), 1), k)
-                pick = (lane_slots[k] == target) & (eighth_lane == eighth_row)
-                pick = jnp.where(pick, 1.0, 0.0).astype(BF16)
-                total = total + jnp.dot(pick, rows_in[k], preferred_element_type=F32)
-            start = j * QUART + half * PART
-            sb[:, :, start : start + PART] = total.astype(BF16).reshape(16, 16, PART)
-
-    own_block = pltpu.make_async_copy(sb.at[expert], rb.at[0, 0], local.at[24])
-    own_block.start()
+    def make_slots(cls):
+        first = lax.rem(zl + CLASSES[cls] + 4, 4) * 64
+        for j in range(3):
+            for half in range(2):
+                target, eighth_row = slot_of(iota((64, 256), 0), j, half)
+                target = (target + first).astype(F32)
+                total = jnp.zeros((64, PART), F32)
+                for k in thirds_for(j, half):
+                    _, eighth_lane = item_of(iota((64, 256), 1), k)
+                    pick = (lane_slots[k] == target) & (eighth_lane == eighth_row)
+                    pick = jnp.where(pick, 1.0, 0.0).astype(BF16)
+                    total = total + jnp.dot(pick, rows_in[k], preferred_element_type=F32)
+                start = j * QUART + half * PART
+                sb[cls, :, :, start : start + PART] = total.astype(BF16).reshape(4, 16, PART)
 
     def parity(cls):
         return lax.rem(y + cls, 2)
@@ -575,11 +574,13 @@
 
     sent = [[], [], [], []]
     for cls in ORDER:
+        make_slots(cls)
         for i, (dz, dx, index) in enumerate(routes(cls)):
-            to = lax.rem(zl + dz + 4, 4) * 4 + lax.rem(x + dx, 4)
-            copy = remote(sb.at[to], rb.at[cls, dx], GO + index, at(dz=dz, dx=dx))
+            copy = remote(sb.at[cls, lax.rem(x + dx, 4)], rb.at[cls, dx], GO + index, at(dz=dz, dx=dx))
             where_sent(cls, i, copy.start)
             sent[cls].append(copy)
+    own_block = pltpu.make_async_copy(sb.at[0, x], rb.at[0, 0], local.at[24])
+    own_block.start()
 
     for copy in copies + weight_copies:
         copy.wait()
@@ -794,7 +795,7 @@
             pltpu.VMEM((8, WIDTH), F32),
             pltpu.VMEM((16, 3 * PART), F32),
             pltpu.VMEM((16, 16, 3 * PART), BF16),
-            pltpu.VMEM(slots, BF16),
+            pltpu.VMEM((4, 4, 16, 3 * QUART), BF16),
             pltpu.VMEM((4, 4, 16, 3 * QUART), BF16),
             pltpu.VMEM((4, 4, 16, 3 * QUART), BF16),
             pltpu.VMEM((4, 2, 16, 3 * QUART), BF16),

time: 129 us -> 129 us (level)
  no operation moved by 1% of the time
where the time goes in v7:
time: 129 us
  Pallas kernels  127 us (98%)
  local copies, waits for them, and re-layouts  1.53 us (1%)
    pallas_call x1, Pallas kernels, body(): pl.pallas_call(kernel, out_shape=jax.ShapeDtypeStruct((1, TOK, WIDTH), BF...  127 us

profile of v7, /device:TPU:8, one launch (start us, length us, event | category | flops | bytes accessed | tf_op | source)
XLA Modules:
  0.0 128.8 jit_solution(15931729365105986879)
XLA Ops:
  0.7 126.6 %shard_map.109 = bf16[1,6,5120]{2,1,0:T(8,128)(2,1)} custom-call(bf16[1,6,5120]{2,1,0:T(8,128)(2,1)} %q_ref.1, bf16[1,6,2,1024]{3,2,1,0:T(2,128)(2,1)} %bitcast.2, bf16[2,1,256,1024]{3,2,1,0:T(8,128)(2,1)} %cache_ref.1, s32[1]{0:T(128)S(6)} %copy.13.len_ref, bf16[1,6,5120]{2,1,0:T(8,128)(2,1)} %res_ref.1, bf16[5120]{0:T(1024)(128)(2,1)} %gain_ref.1, ...), custom_call_target="tpu_custom_call" | custom-call | tf_op jit(solution)/shard_map/pallas_call | solution.py:773
  127.2 1.5 %copy.14 = bf16[1,6,5120]{2,1,0:T(8,128)(2,1)} copy(bf16[1,6,5120]{2,1,0:T(8,128)(2,1)} %shard_map.109) | data formatting | bytes 122880
